TPU v7x, 128 devices: a whole 4x4x4 slice. The times are simulated.
128 devices in a mesh: region: 4 (over x), blk: 32 (over z, y, core).
Axes of the slice: x: 4, y: 4, z: 4, core: 2. Of those that a mesh axis runs over, the one named last changes fastest.
Arguments:
- node_temp: float32 [1048576], P(('region', 'blk')), may hold values from 0.7 to 1.3
- node_diag: float32 [1048576], P(('region', 'blk')), may hold values from 2 to 8
- node_source: float32 [1048576], P(('region', 'blk')), may hold values from 0.5 to 4
- cond_blocks: bfloat16 [4, 32, 192, 128, 128], P('region', 'blk'), may hold values from 7.772446e-05 to 0.0078125
- cond_rows: int32 [4, 32, 192], P('region', 'blk'), may hold values from 0 to 63
- cond_cols: int32 [4, 32, 192], P('region', 'blk'), may hold values from 0 to 65, as said below
- view_blocks: bfloat16 [4, 32, 96, 256, 256], P('region', 'blk'), may hold values from 1.0371208e-05 to 0.010375977
- view_scales: float32 [4, 32, 96, 4], P('region', 'blk'), may hold values from 0.5 to 2
- view_rows: int32 [4, 32, 96], P('region', 'blk'), may hold values from 0 to 511, as said below
- view_cols: int32 [4, 32, 96], P('region', 'blk'), may hold values from 0 to 63
- band_frac: bfloat16 [2048, 4, 256], P(('region', 'blk')), may hold values from 0.099609375 to 0.5
- absorb: bfloat16 [2048, 4, 256], P(('region', 'blk')), may hold values from 0.29882812 to 1
- emis: bfloat16 [2048, 256], P(('region', 'blk')), may hold values from 0.29882812 to 1
- patch_dest: int32 [2048, 256, 1], P(('region', 'blk')), may hold values from 0 to 127; in each aligned block of 4096 rows (0 to 4095, 4096 to 8191, ..., all dimensions but the last counted through in order) at most 64 rows name the same one
- patch_node: int32 [2048, 256], P(('region', 'blk')), may hold values from 0 to 8191
Outputs:
- node_final: float32 [1048576], P(('region', 'blk'))
- patch_flux: float32 [2048, 256], P(('region', 'blk'))
Inputs may be any that keep to these rules, and one draw needn't show every extreme that they name: `patch_dest`: among the patches of one device no device is named more than 64 times, and some device is named exactly 64 times. `cond_cols`: entries 0 and 1 of every device's list are 0 and 65. `view_rows`: among one device's blocks, the rows u with one value of u // 16 hold at most 8 distinct values, and on every device some value of u // 16 has exactly 8.
All inputs are finite; a program needn't handle non-finite values.
Results may differ from a plain program's by a relative error of at most 0.0003.
Values may be sent and summed in bfloat16 or wider, within the bound.
A program may use at most 128 MiB of HBM per device.

v0:
```python
import jax
import jax.numpy as jnp
from jax import lax
from jax.sharding import PartitionSpec as P

ITERS = 2


def with_halo(cells, sides, width):
    for axis, dim in sides:
        count = lax.axis_size(axis)
        ends = count - 1
        head = lax.slice_in_dim(cells, 0, width, axis=dim)
        tail = lax.slice_in_dim(cells, cells.shape[dim] - width, cells.shape[dim], axis=dim)
        cells = jnp.concatenate(
            [
                lax.ppermute(tail, axis, [(i, (i + 1) % count) for i in range(ends)]),
                cells,
                lax.ppermute(head, axis, [((i + 1) % count, i) for i in range(ends)]),
            ],
            axis=dim,
        )
    return cells


def relay_back(answer):
    return lax.all_to_all(answer, ("region", "blk"), split_axis=0, concat_axis=0, tiled=True)


def relay_out(outgoing):
    return lax.all_to_all(outgoing, ("region", "blk"), split_axis=1, concat_axis=1, tiled=True)


def shards(
    node_temp,
    node_diag,
    node_source,
    cond_blocks,
    cond_rows,
    cond_cols,
    view_blocks,
    view_scales,
    view_rows,
    view_cols,
    band_frac,
    absorb,
    emis,
    patch_dest,
    patch_node,
):
    highest = lax.Precision.HIGHEST
    regions = lax.axis_size("region")
    columns = lax.axis_size("blk")
    peer_count = regions * columns
    rb_dev, band_count, block_size = band_frac.shape
    patch_dev = rb_dev * block_size
    capacity = 2 * patch_dev // peer_count
    node_dev = node_temp.shape[0]
    node_block = cond_blocks.shape[-1]
    node_tiles = node_dev // node_block
    region_rows = rb_dev * columns
    group_cols = rb_dev * regions
    destination = patch_dest.reshape(patch_dev)
    local_node = patch_node.reshape(patch_dev)
    sort_order = jnp.argsort(destination, stable=True)
    bucket_count = jnp.sum(
        (destination[:, None] == jnp.arange(peer_count, dtype=jnp.int32)[None, :]).astype(
            jnp.int32
        ),
        axis=0,
    )
    bucket_start = jnp.cumsum(bucket_count) - bucket_count
    sorted_dest = destination[sort_order]
    rank_sorted = jnp.arange(patch_dev, dtype=jnp.int32) - bucket_start[sorted_dest]
    slot_index = jnp.zeros((patch_dev,), jnp.int32).at[sort_order].set(rank_sorted)
    send_place = destination * capacity + slot_index
    requests = jnp.full((peer_count * capacity,), -1, jnp.int32).at[send_place].set(local_node)
    incoming = lax.all_to_all(
        requests.reshape(peer_count, capacity),
        ("region", "blk"),
        split_axis=0,
        concat_axis=0,
        tiled=True,
    )
    filled = (incoming >= 0).astype(jnp.float32).reshape(-1)
    target = jnp.maximum(incoming, 0).reshape(-1)
    blocks = view_blocks.reshape(view_blocks.shape[2:])
    view_count = blocks.shape[0]
    scales = view_scales.reshape(view_scales.shape[2:])
    block_rows = view_rows.reshape(-1)
    block_cols = view_cols.reshape(-1)
    cond_tiles = cond_blocks.reshape(cond_blocks.shape[2:])
    tile_rows = cond_rows.reshape(-1)
    tile_cols = cond_cols.reshape(-1)
    emis_f = emis.astype(jnp.float32)
    row_pick = (block_rows[:, None] == jnp.arange(region_rows, dtype=jnp.int32)[None, :]).astype(
        jnp.float32
    )
    col_pick = (block_cols[:, None] == jnp.arange(group_cols, dtype=jnp.int32)[None, :]).astype(
        jnp.bfloat16
    )
    tile_pick = (tile_cols[:, None] == jnp.arange(node_tiles + 2, dtype=jnp.int32)[None, :]).astype(
        jnp.float32
    )
    tile_place = (tile_rows[:, None] == jnp.arange(node_tiles, dtype=jnp.int32)[None, :]).astype(
        jnp.float32
    )
    node_temps = node_temp
    patch_flux = jnp.zeros((rb_dev, block_size), jnp.float32)
    for iteration in range(ITERS):
        answer = (node_temps[target] * filled).reshape(peer_count, capacity)
        fetched = relay_back(answer)
        patch_temp = fetched.reshape(-1)[send_place].reshape(rb_dev, block_size)
        squared = patch_temp * patch_temp
        quartic = squared * squared
        emit = (band_frac.astype(jnp.float32) * quartic[:, None, :]).astype(jnp.bfloat16)
        column_emit = lax.all_gather(emit, "region", axis=0, tiled=True)
        col_emit = jnp.dot(
            col_pick, column_emit.reshape(group_cols, -1), preferred_element_type=jnp.float32
        ).astype(jnp.bfloat16)
        col_emit = col_emit.reshape(view_count, band_count, block_size)
        products = jnp.einsum("kij,kbj->kbi", blocks, col_emit, preferred_element_type=jnp.float32)
        products = products * scales[:, :, None]
        partial_value = jnp.einsum(
            "kr,kx->rx", row_pick, products.reshape(view_count, -1), precision=highest
        )
        partial_value = partial_value.reshape(region_rows, band_count, block_size)
        band_flux = lax.psum_scatter(partial_value, "blk", scatter_dimension=0, tiled=True)
        gained = jnp.sum(absorb.astype(jnp.float32) * band_flux, axis=1)
        patch_flux = gained - emis_f * quartic
        payload = jnp.stack([patch_flux.reshape(-1), emis_f.reshape(-1)])
        outgoing = jnp.zeros((2, peer_count * capacity), jnp.float32).at[:, send_place].set(payload)
        arrived = relay_out(outgoing.reshape(2, peer_count, capacity)).reshape(2, -1)
        heat = jax.ops.segment_sum(arrived[0], target, num_segments=node_dev)
        emis_sum = jax.ops.segment_sum(arrived[1], target, num_segments=node_dev)
        extended = with_halo(node_temps, ((("region", "blk"), 0),), node_block)
        extended = extended.reshape(node_tiles + 2, node_block)
        col_temps = jnp.einsum("kt,tj->kj", tile_pick, extended, precision=highest)
        upper = col_temps.astype(jnp.bfloat16)
        lower = (col_temps - upper.astype(jnp.float32)).astype(jnp.bfloat16)
        halves = jnp.stack([upper, lower], axis=1)
        cond_parts = jnp.einsum(
            "kij,ksj->ksi", cond_tiles, halves, preferred_element_type=jnp.float32
        )
        cond_terms = cond_parts[:, 0] + cond_parts[:, 1]
        conducted = jnp.einsum("kt,ki->ti", tile_place, cond_terms, precision=highest).reshape(-1)
        residual = node_diag * node_temps - conducted - heat - node_source
        magnitude = jnp.abs(node_temps)
        node_temps = node_temps - residual / (
            node_diag + 4.0 * magnitude * magnitude * magnitude * emis_sum
        )
    return (node_temps, patch_flux)


def solution(mesh):
    placed = (
        P(("region", "blk")),
        P(("region", "blk")),
        P(("region", "blk")),
        P("region", "blk", None, None, None),
        P("region", "blk", None),
        P("region", "blk", None),
        P("region", "blk", None, None, None),
        P("region", "blk", None, None),
        P("region", "blk", None),
        P("region", "blk", None),
        P(("region", "blk"), None, None),
        P(("region", "blk"), None, None),
        P(("region", "blk"), None),
        P(("region", "blk"), None, None),
        P(("region", "blk"), None),
    )
    return jax.shard_map(
        shards,
        mesh=mesh,
        in_specs=placed,
        out_specs=(P(("region", "blk")), P(("region", "blk"), None)),
        check_vma=False,
    )
```

profile of v0, /device:TPU:1, one launch (start us, length us, event | category | flops | bytes accessed | tf_op | source)
XLA Modules:
  0.0 773.4 jit_solution(17760271548065495919)
XLA Ops:
  16.6 23.0 %gather_fusion = s32[4096]{0:T(1024)S(1)} fusion(s32[4096]{0:T(1024)S(1)} %bitcast.135, s32[4096]{0:T(1024)S(1)} %get-tuple-element.20), kind=kCustom, calls=%fused_computation | custom fusion | bytes 49152 | tf_op jit(solution)/shard_map/gather | solution.py:73
  39.7 24.7 %gather_fusion.1 = s32[4096]{0:T(1024)S(1)} fusion(s32[128]{0:T(128)S(1)} %sub.44, s32[4096]{0:T(1024)S(1)} %broadcast_clamp_fusion.2), kind=kCustom, calls=%fused_computation.1 | custom fusion | bytes 49152 | tf_op jit(solution)/shard_map/gather | solution.py:74
  64.5 15.5 %scatter_custom_fusion = s32[4096]{0:T(1024)S(1)} fusion(s32[4096]{0:T(1024)S(1)} %get-tuple-element.21, s32[4096]{0:T(1024)S(1)} %iota_subtract_fusion, s32[]{:T(128)} %constant.11.clone.1), kind=kCustom, calls=%fused_computation.139 | custom fusion | bytes 16388 | tf_op jit(solution)/shard_map/scatter | solution.py:75
  80.0 15.5 %scatter_custom_fusion.1 = s32[8192]{0:T(1024)S(1)} fusion(s32[4096]{0:T(1024)S(1)} %get-tuple-element.9, s32[4096]{0:T(1024)S(1)} %bitcast.163, s32[]{:T(128)} %constant.9.clone.1), kind=kCustom, calls=%fused_computation.126 | custom fusion | bytes 32772 | tf_op jit(solution)/shard_map/scatter | solution.py:77
  95.7 20.8 %all_to_all.31 = s32[128,1,64]{2,1,0:T(1,128)S(1)} all-to-all(s32[128,1,64]{2,1,0:T(1,128)S(1)} %bitcast.154), channel_id=1, replica_groups=mesh['region'=4,'blk'=32] {'region','blk'}, dimensions={0} | all-to-all | bytes 65536 | tf_op jit(solution)/shard_map/all_to_all | solution.py:78
  116.6 45.5 %gather_fusion.2 = f32[8192]{0:T(1024)S(1)} fusion(f32[8192]{0:T(1024)S(1)} %copy-done, s32[8192]{0:T(1024)S(1)} %broadcast_clamp_fusion), kind=kCustom, calls=%fused_computation.2 | custom fusion | bytes 98304 | tf_op jit(solution)/shard_map/gather | solution.py:111
  167.6 9.3 %all-to-all-done.1 = f32[128,1,64]{2,1,0:T(1,128)S(1)} async-done(((f32[128,1,64]{2,1,0:T(1,128)}), f32[128,1,64]{2,1,0:T(1,128)S(1)}, u32[]{:S(2)}, u32[]{:S(2)}) %all-to-all-start.1) | async-done | bytes 32800 | tf_op jit(solution)/shard_map/all_to_all | solution.py:27
  178.4 23.0 %gather_fusion.3 = f32[4096]{0:T(1024)S(1)} fusion(f32[8192]{0:T(1024)S(1)} %reshape.179, s32[4096]{0:T(1024)S(1)} %get-tuple-element.8), kind=kCustom, calls=%fused_computation.3 | custom fusion | bytes 49152 | tf_op jit(solution)/shard_map/gather | solution.py:113
  201.5 9.1 %all_gather.6 = bf16[64,4,256]{2,1,0:T(4,128)(2,1)S(1)} all-gather(bf16[16,4,256]{2,1,0:T(4,128)(2,1)S(1)} %fusion.45), channel_id=1, replica_groups=mesh['region'=4,'blk'=32] {'region'}, dimensions={0}, use_global_device_ids=true | all-gather | bytes 163840 | tf_op jit(solution)/shard_map/all_gather | solution.py:117
  238.6 59.9 %reduce-scatter.3.cloned.1.call-done = f32[16,4,256]{2,0,1:T(8,128)} async-done(((f32[512,4,256]{2,0,1:T(8,128)}), f32[16,4,256]{2,0,1:T(8,128)}) %reduce-scatter.3.cloned.1.call-update) | async-done | bytes 65552 | tf_op jit(solution)/shard_map/reduce_scatter | solution.py:128
  300.2 12.8 %scatter_custom_fusion.2 = f32[2,8192]{0,1:T(8,128)} fusion(s32[4096]{0:T(1024)S(1)} %get-tuple-element.9, f32[4096,2]{1,0:T(8,128)S(1)} %copy.64, f32[]{:T(128)} %constant.8.clone.1), kind=kCustom, calls=%fused_computation.24 | custom fusion | bytes 65540 | tf_op jit(solution)/shard_map/scatter | solution.py:132
  325.9 9.3 %all-to-all-done.2 = f32[128,1,128]{2,1,0:T(1,128)S(1)} async-done(((f32[128,1,128]{2,1,0:T(1,128)}), f32[128,1,128]{2,1,0:T(1,128)S(1)}, u32[]{:S(2)}, u32[]{:S(2)}) %all-to-all-start.2) | async-done | bytes 65568 | tf_op jit(solution)/shard_map/all_to_all | solution.py:31
  337.1 52.3 %scatter_custom_fusion.4 = f32[8192]{0:T(1024)S(1)} fusion(s32[8192]{0:T(1024)S(1)} %reshape.266, f32[8192]{0:T(1024)S(1)} %reshape.276, f32[]{:T(128)} %constant.8.clone.1), kind=kCustom, calls=%fused_computation.132 | custom fusion | flops 8192 | bytes 32772 | tf_op jit(solution)/shard_map/scatter-add | solution.py:135
  389.5 52.3 %scatter_custom_fusion.3 = f32[8192]{0:T(1024)S(1)} fusion(s32[8192]{0:T(1024)S(1)} %reshape.266, f32[8192]{0:T(1024)S(1)} %reshape.268, f32[]{:T(128)} %constant.8.clone.1), kind=kCustom, calls=%fused_computation.134 | custom fusion | flops 8192 | bytes 32772 | tf_op jit(solution)/shard_map/scatter-add | solution.py:134
  442.1 45.5 %gather_fusion.4 = f32[8192]{0:T(1024)S(1)} fusion(f32[8192]{0:T(1024)S(1)} %fusion.22, s32[8192]{0:T(1024)S(1)} %broadcast_clamp_fusion), kind=kCustom, calls=%fused_computation.4 | custom fusion | bytes 98304 | tf_op jit(solution)/shard_map/gather | solution.py:111
  487.8 13.8 %all_to_all.32 = f32[128,1,64]{2,1,0:T(1,128)S(1)} all-to-all(f32[128,1,64]{2,1,0:T(1,128)S(1)} %bitcast.153), channel_id=1, replica_groups=mesh['region'=4,'blk'=32] {'region','blk'}, dimensions={0} | all-to-all | bytes 65536 | tf_op jit(solution)/shard_map/all_to_all | solution.py:27
  502.5 23.0 %gather_fusion.5 = f32[4096]{0:T(1024)S(1)} fusion(f32[8192]{0:T(1024)S(1)} %reshape.187, s32[4096]{0:T(1024)S(1)} %get-tuple-element.8), kind=kCustom, calls=%fused_computation.5 | custom fusion | bytes 49152 | tf_op jit(solution)/shard_map/gather | solution.py:113
  525.6 9.3 %all_gather.7 = bf16[64,4,256]{2,1,0:T(4,128)(2,1)S(1)} all-gather(bf16[16,4,256]{2,1,0:T(4,128)(2,1)S(1)} %fusion.46), channel_id=1, replica_groups=mesh['region'=4,'blk'=32] {'region'}, dimensions={0}, use_global_device_ids=true | all-gather | bytes 163840 | tf_op jit(solution)/shard_map/all_gather | solution.py:117
  562.9 59.9 %reduce-scatter.5.cloned.1.call-done = f32[16,4,256]{2,0,1:T(8,128)} async-done(((f32[512,4,256]{2,0,1:T(8,128)}), f32[16,4,256]{2,0,1:T(8,128)}) %reduce-scatter.5.cloned.1.call-update) | async-done | bytes 65552 | tf_op jit(solution)/shard_map/reduce_scatter | solution.py:128
  624.4 12.8 %scatter_custom_fusion.5 = f32[2,8192]{0,1:T(8,128)} fusion(s32[4096]{0:T(1024)S(1)} %get-tuple-element.9, f32[4096,2]{1,0:T(8,128)S(1)} %copy.69, f32[]{:T(128)} %constant.8.clone.1), kind=kCustom, calls=%fused_computation.22 | custom fusion | bytes 65540 | tf_op jit(solution)/shard_map/scatter | solution.py:132
  641.0 9.1 %all-to-all-start.4 = ((f32[128,1,128]{2,1,0:T(1,128)}), f32[128,1,128]{2,1,0:T(1,128)S(1)}, u32[]{:S(2)}, u32[]{:S(2)}) async-start(f32[128,1,128]{2,1,0:T(1,128)} %reshape.373), calls=%async_computation.6 | async-start | bytes 131072 | tf_op jit(solution)/shard_map/all_to_all | solution.py:31
  650.2 9.4 %all-to-all-done.4 = f32[128,1,128]{2,1,0:T(1,128)S(1)} async-done(((f32[128,1,128]{2,1,0:T(1,128)}), f32[128,1,128]{2,1,0:T(1,128)S(1)}, u32[]{:S(2)}, u32[]{:S(2)}) %all-to-all-start.4) | async-done | bytes 65568 | tf_op jit(solution)/shard_map/all_to_all | solution.py:31
  661.0 52.3 %scatter_custom_fusion.7 = f32[8192]{0:T(1024)S(1)} fusion(s32[8192]{0:T(1024)S(1)} %reshape.266, f32[8192]{0:T(1024)S(1)} %reshape.300, f32[]{:T(128)} %constant.8.clone.1), kind=kCustom, calls=%fused_computation.128 | custom fusion | flops 8192 | bytes 32772 | tf_op jit(solution)/shard_map/scatter-add | solution.py:135
  713.3 52.3 %scatter_custom_fusion.6 = f32[8192]{0:T(1024)S(1)} fusion(s32[8192]{0:T(1024)S(1)} %reshape.266, f32[8192]{0:T(1024)S(1)} %reshape.292, f32[]{:T(128)} %constant.8.clone.1), kind=kCustom, calls=%fused_computation.130 | custom fusion | flops 8192 | bytes 32772 | tf_op jit(solution)/shard_map/scatter-add | solution.py:134
  (124 shorter events, 98.0 us)
Async XLA Ops:
  7.2 9.5 %copy-start.1 = (s32[16,256,1]{1,2,0:T(1,128)S(1)}, s32[16,256,1]{1,2,0:T(1,128)}, u32[]{:S(2)}) copy-start(s32[16,256,1]{1,2,0:T(1,128)} %param.28) | copy-start | bytes 49156
  39.7 40.3 %copy-start.8 = (s32[16,256]{1,0:T(8,128)S(1)}, s32[16,256]{1,0:T(8,128)}, u32[]{:S(2)}) copy-start(s32[16,256]{1,0:T(8,128)} %param.29) | copy-start | bytes 49156
  64.4 52.1 %copy-start = (f32[8192]{0:T(1024)S(1)}, f32[8192]{0:T(1024)}, u32[]{:S(2)}) copy-start(f32[8192]{0:T(1024)} %param.15) | copy-start | bytes 98308
  116.6 50.9 %copy-start.12 = (f32[1,1,96,4]{2,3,1,0:T(4,128)S(1)}, f32[1,1,96,4]{2,3,1,0:T(4,128)}, u32[]{:S(2)}) copy-start(f32[1,1,96,4]{2,3,1,0:T(4,128)} %param.22) | copy-start | bytes 4612
  162.8 14.1 %all-to-all-start.1 = ((f32[128,1,64]{2,1,0:T(1,128)}), f32[128,1,64]{2,1,0:T(1,128)S(1)}, u32[]{:S(2)}, u32[]{:S(2)}) async-start(f32[128,1,64]{2,1,0:T(1,128)} %bitcast.18), calls=%async_computation.1 | async-start | bytes 131072 | tf_op jit(solution)/shard_map/all_to_all | solution.py:27
  167.4 131.1 %reduce-scatter.3.cloned.1.call-start = ((), (), s32[]{:S(2)}) async-start(), calls=%async_computation.7 | async-start | bytes 2162688 | tf_op jit(solution)/shard_map/reduce_scatter | solution.py:128
  178.3 23.1 %copy-start.5 = (bf16[16,4,256]{2,1,0:T(4,128)(2,1)S(1)}, bf16[16,4,256]{2,1,0:T(4,128)(2,1)}, u32[]{:S(2)}) copy-start(bf16[16,4,256]{2,1,0:T(4,128)(2,1)} %param.25) | copy-start | bytes 98308
  178.4 32.2 %copy-start.11 = (s32[1,1,96]{2,1,0:T(1,128)S(1)}, s32[1,1,96]{2,1,0:T(1,128)}, u32[]{:S(2)}) copy-start(s32[1,1,96]{2,1,0:T(1,128)} %param.24) | copy-start | bytes 1156
  211.0 8.0 %copy-start.13 = (s32[1,1,96]{2,1,0:T(1,128)S(1)}, s32[1,1,96]{2,1,0:T(1,128)}, u32[]{:S(2)}) copy-start(s32[1,1,96]{2,1,0:T(1,128)} %param.23) | copy-start | bytes 1156
  218.9 10.5 %copy-start.6 = (bf16[16,256]{1,0:T(8,128)(2,1)S(1)}, bf16[16,256]{1,0:T(8,128)(2,1)}, u32[]{:S(2)}) copy-start(bf16[16,256]{1,0:T(8,128)(2,1)} %param.27) | copy-start | bytes 24580
  218.9 13.2 %copy-start.9 = (s32[1,1,192]{2,1,0:T(1,128)S(1)}, s32[1,1,192]{2,1,0:T(1,128)}, u32[]{:S(2)}) copy-start(s32[1,1,192]{2,1,0:T(1,128)} %param.20) | copy-start | bytes 2308
  221.4 77.1 %copy-start.2 = (bf16[16,4,256]{2,1,0:T(4,128)(2,1)S(1)}, bf16[16,4,256]{2,1,0:T(4,128)(2,1)}, u32[]{:S(2)}) copy-start(bf16[16,4,256]{2,1,0:T(4,128)(2,1)} %param.26) | copy-start | bytes 98308
  221.4 8.0 %collective-permute-start = (f32[128]{0:T(128)S(1)}, f32[128]{0:T(128)S(1)}, u32[]{:S(2)}, u32[]{:S(2)}) collective-permute-start(f32[128]{0:T(128)S(1)} %get-tuple-element.18), channel_id=1, source_target_pairs={{0,1},{1,2},{2,3},{3,4},{4,5},{5,6},{6,7},{7,8},{8,9},{9,10},{10,1... | collective-permute-start | bytes 1544 | tf_op jit(solution)/shard_map/ppermute | solution.py:17
  227.3 4.9 collective-permute-start.1
  300.1 141.6 %copy-start.3 = (f32[8192]{0:T(1024)S(1)}, f32[8192]{0:T(1024)}, u32[]{:S(2)}) copy-start(f32[8192]{0:T(1024)} %param.17) | copy-start | bytes 98308
  300.1 141.6 %copy-start.4 = (f32[8192]{0:T(1024)S(1)}, f32[8192]{0:T(1024)}, u32[]{:S(2)}) copy-start(f32[8192]{0:T(1024)} %param.16) | copy-start | bytes 98308
  300.2 141.6 %copy-start.10 = (s32[1,1,192]{2,1,0:T(1,128)S(1)}, s32[1,1,192]{2,1,0:T(1,128)}, u32[]{:S(2)}) copy-start(s32[1,1,192]{2,1,0:T(1,128)} %param.19) | copy-start | bytes 2308
  316.7 18.5 %all-to-all-start.2 = ((f32[128,1,128]{2,1,0:T(1,128)}), f32[128,1,128]{2,1,0:T(1,128)S(1)}, u32[]{:S(2)}, u32[]{:S(2)}) async-start(f32[128,1,128]{2,1,0:T(1,128)} %reshape.371), calls=%async_computation.3 | async-start | bytes 131072 | tf_op jit(solution)/shard_map/all_to_all | solution.py:31
  325.7 297.1 %reduce-scatter.5.cloned.1.call-start = ((), (), s32[]{:S(2)}) async-start(), calls=%async_computation.8 | async-start | bytes 2162688 | tf_op jit(solution)/shard_map/reduce_scatter | solution.py:128
  545.7 7.8 %collective-permute-start.2 = (f32[128]{0:T(128)S(1)}, f32[128]{0:T(128)S(1)}, u32[]{:S(2)}, u32[]{:S(2)}) collective-permute-start(f32[128]{0:T(128)S(1)} %get-tuple-element.16), channel_id=1, source_target_pairs={{0,1},{1,2},{2,3},{3,4},{4,5},{5,6},{6,7},{7,8},{8,9},{9,10},{10,1... | collective-permute-start | bytes 1544 | tf_op jit(solution)/shard_map/ppermute | solution.py:17
  551.6 4.9 collective-permute-start.3
  623.7 16.5 %copy-start.7 = (f32[16,256]{1,0:T(8,128)}, f32[16,256]{1,0:T(8,128)S(1)}, u32[]{:S(2)}) copy-start(f32[16,256]{1,0:T(8,128)S(1)} %fusion.71) | copy-start | bytes 49156
  641.0 18.6 %all-to-all-start.4 = ((f32[128,1,128]{2,1,0:T(1,128)}), f32[128,1,128]{2,1,0:T(1,128)S(1)}, u32[]{:S(2)}, u32[]{:S(2)}) async-start(f32[128,1,128]{2,1,0:T(1,128)} %reshape.373), calls=%async_computation.6 | async-start | bytes 131072 | tf_op jit(solution)/shard_map/all_to_all | solution.py:31
Sparse Core Ops, SparseCore 0:
  221.5 76.9 reduce-scatter.2
  545.9 76.9 reduce-scatter.4
where the time goes:
time: 773 us
  local copies, waits for them, and re-layouts  254 us (33%)
  other arithmetic  224 us (29%)
  waiting for transfers between devices  154 us (20%)
  blocking collectives  53.1 us (7%)
  starting transfers between devices  38.5 us (5%)
  matrix products  35.4 us (5%)
  between operations  14.7 us (2%)
    reduce_scatter x2, waiting for transfers between devices, shards(): lax.psum_scatter(partial_value, 'blk', scatter_dimension=0, tiled=True)  120 us
    scatter-add x2, other arithmetic, shards(): emis_sum = jax.ops.segment_sum(arrived[1], target, num_segments=node_dev)  105 us
    scatter-add x2, other arithmetic, shards(): heat = jax.ops.segment_sum(arrived[0], target, num_segments=node_dev)  105 us
    gather x4, local copies, waits for them, and re-layouts, shards(): answer = (node_temps[target] * filled).reshape(peer_count, capacity)  91.2 us
    gather x2, local copies, waits for them, and re-layouts, shards(): patch_temp = fetched.reshape(-1)[send_place].reshape(rb_dev, block_size)  46.1 us
    scatter x2, local copies, waits for them, and re-layouts, shards(): jnp.zeros((2, peer_count * capacity), jnp.float32).at[:, send_place]  25.5 us
    gather x1, local copies, waits for them, and re-layouts, shards(): bucket_start[sorted_dest]  24.7 us
    gather x1, local copies, waits for them, and re-layouts, shards(): sorted_dest = destination[sort_order]  23 us
  transfers between devices with their start and end apart: 9, of which 7 were waited for; matrix products, arithmetic and copies ran while one was open for 2% of the time, Pallas kernels for 0%

commit v1 on v0

v1 whole, which is shorter than its diff:
```python
import functools

import jax
import jax.numpy as jnp
from jax import lax
from jax.experimental import pallas as pl
from jax.experimental.pallas import tpu as pltpu
from jax.sharding import PartitionSpec as P

ITERS = 2
REGIONS = 4
COLUMNS = 32
PEERS = REGIONS * COLUMNS
BANDS = 4
RB = 16
VIEW = 256
VIEWS = 96
KPAD = 128
GROUP = RB * REGIONS
SLOTS = 8
CAP = 64
TILES = 64
TILE = 128
CONDS = 192
CPAD = 256
MESH = pl.DeviceIdType.MESH
F32 = jnp.float32
BF16 = jnp.bfloat16
I32 = jnp.int32


def mm(a, b):
    return jnp.dot(a, b, preferred_element_type=F32)


def mm_nt(a, b):
    return lax.dot_general(a, b, (((1,), (1,)), ((), ())), preferred_element_type=F32)


def mm_tn(a, b):
    return lax.dot_general(a, b, (((0,), (0,)), ((), ())), preferred_element_type=F32)


def iota(shape, dim):
    return lax.broadcasted_iota(I32, shape, dim)


def pick(mask):
    return jnp.where(mask, 1.0, 0.0).astype(BF16)


def halves(x):
    upper = x.astype(BF16)
    return upper, (x - upper.astype(F32)).astype(BF16)


def rows_to_slots(left, swap):
    low = iota((COLUMNS, 128), 1) < CAP
    part = [left[i * COLUMNS : (i + 1) * COLUMNS] for i in range(REGIONS)]
    pairs = []
    for i in range(0, REGIONS, 2):
        first, second = part[i], part[i + 1]
        if swap:
            first = pltpu.roll(first, CAP, 1)
        else:
            second = pltpu.roll(second, CAP, 1)
        pairs.append(jnp.where(low, first, second))
    return jnp.concatenate(pairs, axis=1)


def kernel(
    temp_ref,
    diag_ref,
    source_ref,
    crow_ref,
    ccol_ref,
    scale_ref,
    vrow_ref,
    vcol_ref,
    frac_ref,
    absorb_ref,
    emis_ref,
    dest_ref,
    node_ref,
    cond_hbm,
    view_hbm,
    node_out,
    flux_out,
    cb,
    vb,
    ohd,
    ohlo,
    code_mine,
    code_all,
    frac_mine,
    frac_all,
    req_send,
    req_recv,
    ans_send,
    ans_recv,
    ab_send,
    ab_recv,
    g_send,
    g_recv,
    f_send,
    f_recv,
    halo_send,
    halo_recv,
    temps,
    emf,
    hi4,
    lo4,
    em4,
    fh4,
    fl4,
    patchq,
    ftl,
    ecol,
    prod,
    abk,
    ohslot,
    colt,
    terms,
    esum,
    pads,
    scalep,
    load_sem,
    setup_send,
    setup_recv,
    ans_ssem,
    ans_rsem,
    g_ssem,
    g_rsem,
    f_ssem,
    f_rsem,
    halo_ssem,
    halo_rsem,
):
    r = lax.axis_index("region")
    c = lax.axis_index("blk")
    me = r * COLUMNS + c

    def peer(i):
        p = jnp.bitwise_xor(me, i)
        return p, (lax.shift_right_logical(p, 5), jnp.bitwise_and(p, COLUMNS - 1))

    def push(src, dst, ssem, rsem, where):
        pltpu.make_async_remote_copy(
            src_ref=src,
            dst_ref=dst,
            send_sem=ssem,
            recv_sem=rsem,
            device_id=where,
            device_id_type=MESH,
        ).start()

    def drain(ref, sem):
        pltpu.make_async_copy(ref, ref, sem).wait()

    cond_load = pltpu.make_async_copy(cond_hbm, cb, load_sem.at[0])
    view_load = pltpu.make_async_copy(view_hbm, vb, load_sem.at[1])
    cond_load.start()
    view_load.start()

    barrier = pltpu.get_barrier_semaphore()

    def greet(i, carry):
        pl.semaphore_signal(barrier, inc=1, device_id=peer(i)[1], device_id_type=MESH)
        return carry

    lax.fori_loop(1, PEERS, greet, 0)

    temps[...] = temp_ref[...]
    emf[...] = emis_ref[...].astype(F32)
    upper_tri = pick(iota((VIEW, VIEW), 0) < iota((VIEW, VIEW), 1))
    peer_row = iota((PEERS, VIEW), 0)
    slot_row = iota((2 * CAP, VIEW), 0)
    slot_rank = jnp.bitwise_and(slot_row, CAP - 1)
    slot_low = slot_row < CAP

    def route(u, carry):
        count, first, second = carry
        dest = dest_ref[pl.ds(u, 1), :]
        node = node_ref[pl.ds(u, 1), :]
        hit = jnp.where(peer_row == dest, 1.0, 0.0)
        hit16 = hit.astype(BF16)
        before = mm(hit16, upper_tri)
        rank = jnp.sum(hit * (before + count), axis=0, keepdims=True).astype(I32)
        code_mine[pl.ds(u, 1), :] = dest * CAP + rank
        high = (lax.shift_right_logical(node, 7) + 1).astype(F32)
        low = jnp.bitwise_and(node, TILE - 1).astype(F32)
        match = slot_rank == rank
        one = jnp.where(match, jnp.where(slot_low, high, emf[pl.ds(u, 1), :]), 0.0)
        two = jnp.where(match & slot_low, low, 0.0)
        first = first + mm_nt(hit16, one.astype(BF16))
        second = second + mm_nt(hit16, two.astype(BF16))
        count = count + hit[:, VIEW - 1 :] + before[:, VIEW - 1 :]
        return count, first, second

    zero_rows = jnp.zeros((PEERS, 2 * CAP), F32)
    _, first, second = lax.fori_loop(
        0, RB, route, (jnp.zeros((PEERS, 1), F32), zero_rows, zero_rows), unroll=2
    )
    lane_low = iota((PEERS, 2 * CAP), 1) < CAP
    req_send[:, 0, :] = first * jnp.where(lane_low, 128.0, 1.0) + second
    req_send[:, 1, :] = zero_rows

    pads[...] = jnp.full((8, CPAD), -1, I32)
    pads[0:1, 0:VIEWS] = vrow_ref[...]
    pads[1:2, 0:VIEWS] = vcol_ref[...]
    pads[2:3, 0:CONDS] = crow_ref[...]
    pads[3:4, 0:CONDS] = ccol_ref[...]
    vrow = pads[0:1, 0:KPAD]
    vcol = pads[1:2, 0:KPAD]
    crow = pads[2:3, :]
    ccol = pads[3:4, :]
    owner = lax.shift_right_arithmetic(vrow, 4)
    offset = jnp.bitwise_and(vrow, RB - 1)
    owner_hit = pick(iota((COLUMNS, KPAD), 0) == owner)
    offset_hit = jnp.where(iota((128, KPAD), 0) == offset, 1.0, 0.0)
    present = jnp.where(mm_nt(owner_hit, offset_hit.astype(BF16)) > 0.5, 1.0, 0.0)
    tri128 = pick(iota((128, 128), 0) < iota((128, 128), 1))
    place = mm(present.astype(BF16), tri128)
    place_of = mm_tn(place.astype(BF16), owner_hit)
    slot = owner * SLOTS + jnp.sum(offset_hit * place_of, axis=0, keepdims=True).astype(I32)
    ohslot[...] = pick(iota((COLUMNS * SLOTS, KPAD), 0) == slot)
    slot_lane = iota((COLUMNS, 128), 1)
    lane_slot = jnp.bitwise_and(slot_lane, SLOTS - 1).astype(F32)
    table = jnp.zeros((COLUMNS, 128), F32)
    for f in range(RB):
        held = jnp.where(present[:, f : f + 1] > 0.5, place[:, f : f + 1], -1.0)
        table = table + jnp.where(lane_slot == held, f + 1.0, 0.0)
    own_lanes = lax.shift_right_logical(slot_lane, 3) == jnp.bitwise_and(c, 15)
    req_send[pl.ds(r * COLUMNS, COLUMNS), 1, :] = jnp.where(own_lanes, table, 0.0)

    for b in range(BANDS):
        frac_mine[b] = frac_ref[:, b, :]
    ohcol = pick(iota((GROUP, KPAD), 0) == vcol)
    scalep[...] = jnp.zeros((KPAD, BANDS), F32)
    scalep[0:VIEWS, :] = scale_ref[...]
    terms[...] = jnp.zeros((CPAD, TILE), F32)
    oh_ctile = pick(iota((TILES, CPAD), 0) == crow)
    ccol_at = jnp.where(ccol == 0, TILES, jnp.where(ccol == TILES + 1, TILES + 1, ccol - 1))
    oh_ccol = pick(iota((TILES + 16, CPAD), 0) == jnp.where(ccol < 0, -1, ccol_at))

    pl.semaphore_wait(barrier, PEERS - 1)

    def send_request(i, carry):
        p, where = peer(i)
        push(req_send.at[p], req_recv.at[me], setup_send.at[0], setup_recv.at[0], where)
        return carry

    lax.fori_loop(1, PEERS, send_request, 0)
    req_recv[pl.ds(me, 1)] = req_send[pl.ds(me, 1)]
    mine = pl.ds(pl.multiple_of(r * RB, RB), RB)
    for i in range(1, REGIONS):
        where = (jnp.bitwise_xor(r, i), c)
        push(code_mine, code_all.at[mine], setup_send.at[1], setup_recv.at[1], where)
        push(frac_mine, frac_all.at[:, mine, :], setup_send.at[2], setup_recv.at[2], where)
    code_all[mine, :] = code_mine[...]
    frac_all[:, mine, :] = frac_mine[...]

    after = lax.rem(me + 1, PEERS)
    ahead = lax.rem(me + PEERS - 1, PEERS)
    after_id = (lax.shift_right_logical(after, 5), jnp.bitwise_and(after, COLUMNS - 1))
    ahead_id = (lax.shift_right_logical(ahead, 5), jnp.bitwise_and(ahead, COLUMNS - 1))

    def send_halo(it):
        halo_send[it, 0] = temps[TILES - 1 :, :]
        halo_send[it, 1] = temps[0:1, :]
        push(
            halo_send.at[it, 0], halo_recv.at[it, 0], halo_ssem.at[it, 0], halo_rsem.at[it, 0], after_id
        )
        push(
            halo_send.at[it, 1], halo_recv.at[it, 1], halo_ssem.at[it, 1], halo_rsem.at[it, 1], ahead_id
        )

    def wait_halo(it):
        for s in range(2):
            drain(halo_recv.at[it, s], halo_rsem.at[it, s])
            drain(halo_send.at[it, s], halo_ssem.at[it, s])

    send_halo(0)

    others = pl.ds(0, (REGIONS - 1) * RB)
    drain(code_all.at[others], setup_recv.at[1])
    drain(code_all.at[others], setup_send.at[1])

    def build_dest(q, carry):
        ohd[q] = pick(peer_row == lax.shift_right_logical(code_all[pl.ds(q, 1), :], 6))
        return carry

    lax.fori_loop(0, GROUP, build_dest, 0, unroll=4)
    drain(frac_all.at[:, others, :], setup_recv.at[2])
    drain(frac_all.at[:, others, :], setup_send.at[2])

    drain(req_recv.at[0 : PEERS - 1], setup_recv.at[0])
    drain(req_recv.at[0 : PEERS - 1], setup_send.at[0])
    asked = req_recv[:, 0, :]
    code4 = rows_to_slots(asked, False).astype(I32)
    em4[...] = rows_to_slots(asked, True)
    hi4[...] = lax.shift_right_logical(code4, 7) - 1
    lo4[...] = jnp.bitwise_and(code4, TILE - 1)
    tile_row = iota((TILES, VIEW), 0)
    node_row = iota((TILE, VIEW), 0)

    def build_node(j, carry):
        ohlo[j] = pick(node_row == lo4[pl.ds(j, 1), :])
        return carry

    lax.fori_loop(0, COLUMNS, build_node, 0, unroll=4)

    def answer(it):
        up, down = halves(temps[...])
        both = jnp.concatenate([up, down], axis=0)

        def look(j, carry):
            found = mm(both, ohlo[j])
            found = found[0:TILES] + found[TILES:]
            ans_send[j] = jnp.sum(
                jnp.where(tile_row == hi4[pl.ds(j, 1), :], found, 0.0), axis=0, keepdims=True
            )
            return carry

        lax.fori_loop(0, COLUMNS, look, 0, unroll=8)

        def send(i, carry):
            p, where = peer(i)
            push(ans_send.at[where[1]], ans_recv.at[it, me], ans_ssem.at[it], ans_rsem.at[it], where)
            return carry

        lax.fori_loop(1, PEERS, send, 0)
        ans_recv[it, pl.ds(me, 1)] = ans_send[pl.ds(c, 1)]

    def conduct(it):
        wait_halo(it)
        before = jnp.where(me == 0, 0.0, halo_recv[it, 0])
        behind = jnp.where(me == PEERS - 1, 0.0, halo_recv[it, 1])
        edge_row = iota((16, TILE), 0)
        edges = jnp.where(edge_row == 0, before, jnp.where(edge_row == 1, behind, 0.0))
        up, down = halves(jnp.concatenate([temps[...], edges], axis=0))
        colt[...] = mm_tn(oh_ccol, jnp.concatenate([up, down], axis=1))
        eight = iota((8, TILE), 0)

        def group(g, carry):
            rows = colt[pl.ds(pl.multiple_of(g * 8, 8), 8), :]
            left = jnp.concatenate([rows[:, 0:TILE], rows[:, TILE:]], axis=0).astype(BF16)
            total = jnp.zeros((8, TILE), F32)
            for a in range(8):
                part = mm_nt(left, cb[g * 8 + a])
                total = jnp.where(eight == a, part[0:8] + part[8:16], total)
            terms[pl.ds(pl.multiple_of(g * 8, 8), 8), :] = total
            return carry

        lax.fori_loop(0, CONDS // 8, group, 0)
        up, down = halves(terms[...])
        return mm(oh_ctile, up) + mm(oh_ctile, down)

    answer(0)

    codes = req_recv[pl.ds(r * COLUMNS, COLUMNS), 1, :]
    row_codes = jnp.concatenate(
        [
            jnp.sum(codes[0:16], axis=0, keepdims=True),
            jnp.sum(codes[16:32], axis=0, keepdims=True),
        ],
        axis=1,
    ).astype(I32)
    ohrow = pick(iota((RB, COLUMNS * SLOTS), 0) + 1 == row_codes)
    for b in range(0, BANDS, 2):
        pair = [
            mm_tn(ohrow, absorb_ref[:, b + i, :]).reshape(COLUMNS, SLOTS, VIEW) for i in range(2)
        ]
        ab_send[:, b * SLOTS : (b + 2) * SLOTS, :] = jnp.concatenate(pair, axis=1).astype(BF16)

    def send_absorb(i, carry):
        p = jnp.bitwise_xor(c, i)
        push(ab_send.at[p], ab_recv.at[c], setup_send.at[3], setup_recv.at[3], (r, p))
        return carry

    lax.fori_loop(1, COLUMNS, send_absorb, 0)
    ab_recv[pl.ds(c, 1)] = ab_send[pl.ds(c, 1)]

    def gather_emis(j, acc):
        spread = jnp.where(tile_row == hi4[pl.ds(j, 1), :], em4[pl.ds(j, 1), :], 0.0)
        return acc + mm_nt(spread.astype(BF16), ohlo[j])

    esum[...] = lax.fori_loop(0, COLUMNS, gather_emis, jnp.zeros((TILES, TILE), F32), unroll=4)

    rank_row = iota((CAP, VIEW), 0)

    for it in range(ITERS):
        if it > 0:
            answer(it)
        drain(ans_recv.at[it, 0 : PEERS - 1], ans_rsem.at[it])
        drain(ans_recv.at[it, 0 : PEERS - 1], ans_ssem.at[it])
        up, down = halves(ans_recv[it, :, 0, :].T)
        for i in range(REGIONS):
            span = slice(i * CAP, (i + 1) * CAP)
            ftl[i] = jnp.concatenate([up[span], down[span]], axis=0)

        def unpack(q, carry):
            found = mm(ftl[lax.shift_right_logical(q, 4)], ohd[q])
            found = found[0:CAP] + found[CAP:]
            rank = jnp.bitwise_and(code_all[pl.ds(q, 1), :], CAP - 1)
            value = jnp.sum(jnp.where(rank_row == rank, found, 0.0), axis=0, keepdims=True)
            squared = value * value
            patchq[pl.ds(q, 1), :] = squared * squared
            return carry

        lax.fori_loop(0, GROUP, unpack, 0, unroll=8)
        quartic = patchq[...]
        for b in range(BANDS):
            emit = (frac_all[b].astype(F32) * quartic).astype(BF16)
            ecol[b] = mm_tn(ohcol, emit)
        if it == 0:
            view_load.wait()

        def view(k, carry):
            prod[:, k, :] = mm_nt(ecol[:, k, :].astype(BF16), vb[k])
            return carry

        lax.fori_loop(0, VIEWS, view, 0, unroll=8)
        if it == 0:
            drain(ab_recv.at[0 : COLUMNS - 1], setup_recv.at[3])
            drain(ab_recv.at[0 : COLUMNS - 1], setup_send.at[3])
            rows = ab_recv[...].astype(F32)
            for b in range(BANDS):
                mine_b = rows[:, b * SLOTS : (b + 1) * SLOTS, :].reshape(COLUMNS * SLOTS, VIEW)
                abk[b] = mm_tn(ohslot[...], mine_b.astype(BF16)) * scalep[:, b : b + 1]
        gained = prod[0] * abk[0, 0:VIEWS]
        for b in range(1, BANDS):
            gained = gained + prod[b] * abk[b, 0:VIEWS]
        up, down = halves(
            jnp.concatenate([gained, jnp.zeros((KPAD - VIEWS, VIEW), F32)], axis=0)
        )
        g_send[...] = (mm(ohslot[...], up) + mm(ohslot[...], down)).reshape(COLUMNS, SLOTS, VIEW)

        def send_rows(i, carry):
            p = jnp.bitwise_xor(c, i)
            push(g_send.at[p], g_recv.at[it, c], g_ssem.at[it], g_rsem.at[it], (r, p))
            return carry

        lax.fori_loop(1, COLUMNS, send_rows, 0)
        g_recv[it, pl.ds(c, 1)] = g_send[pl.ds(c, 1)]
        if it == 0:
            cond_load.wait()
        conducted = conduct(it)
        drain(g_recv.at[it, 0 : COLUMNS - 1], g_rsem.at[it])
        drain(g_recv.at[it, 0 : COLUMNS - 1], g_ssem.at[it])
        up, down = halves(g_recv[it].reshape(COLUMNS * SLOTS, VIEW))
        flux = mm(ohrow, up) + mm(ohrow, down) - emf[...] * patchq[mine, :]
        flux_out[...] = flux
        up, down = halves(flux)
        up, down = up.astype(F32), down.astype(F32)
        packed = jnp.zeros((PEERS, 2 * CAP), F32)
        for u in range(RB):
            rank = jnp.bitwise_and(code_mine[u : u + 1, :], CAP - 1)
            spread = jnp.where(
                slot_rank == rank, jnp.where(slot_low, up[u : u + 1], down[u : u + 1]), 0.0
            )
            packed = packed + mm_nt(ohd[r * RB + u], spread.astype(BF16))
        f_send[:, 0, :] = packed

        def send_flux(i, carry):
            p, where = peer(i)
            push(f_send.at[p], f_recv.at[it, me], f_ssem.at[it], f_rsem.at[it], where)
            return carry

        lax.fori_loop(1, PEERS, send_flux, 0)
        f_recv[it, pl.ds(me, 1)] = f_send[pl.ds(me, 1)]
        drain(f_recv.at[it, 0 : PEERS - 1], f_rsem.at[it])
        drain(f_recv.at[it, 0 : PEERS - 1], f_ssem.at[it])
        came = f_recv[it, :, 0, :]
        fh4[...] = rows_to_slots(came, False)
        fl4[...] = rows_to_slots(came, True)

        def gather_heat(j, acc):
            hit = tile_row == hi4[pl.ds(j, 1), :]
            spread = jnp.concatenate(
                [
                    jnp.where(hit, fh4[pl.ds(j, 1), :], 0.0).astype(BF16),
                    jnp.where(hit, fl4[pl.ds(j, 1), :], 0.0).astype(BF16),
                ],
                axis=0,
            )
            return acc + mm_nt(spread, ohlo[j])

        heat = lax.fori_loop(
            0, COLUMNS, gather_heat, jnp.zeros((2 * TILES, TILE), F32), unroll=4
        )
        old = temps[...]
        residual = (
            diag_ref[...] * old - conducted - (heat[0:TILES] + heat[TILES:]) - source_ref[...]
        )
        magnitude = jnp.abs(old)
        new = old - residual / (
            diag_ref[...] + 4.0 * magnitude * magnitude * magnitude * esum[...]
        )
        if it + 1 < ITERS:
            temps[...] = new
            send_halo(it + 1)
        else:
            node_out[...] = new


def shards(
    node_temp,
    node_diag,
    node_source,
    cond_blocks,
    cond_rows,
    cond_cols,
    view_blocks,
    view_scales,
    view_rows,
    view_cols,
    band_frac,
    absorb,
    emis,
    patch_dest,
    patch_node,
):
    vmem = pl.BlockSpec(memory_space=pltpu.VMEM)
    hbm = pl.BlockSpec(memory_space=pl.ANY)
    dma = pltpu.SemaphoreType.DMA
    node_final, patch_flux = pl.pallas_call(
        kernel,
        out_shape=(
            jax.ShapeDtypeStruct((TILES, TILE), F32),
            jax.ShapeDtypeStruct((RB, VIEW), F32),
        ),
        in_specs=[vmem] * 13 + [hbm] * 2,
        out_specs=(vmem, vmem),
        scratch_shapes=[
            pltpu.VMEM((CONDS, TILE, TILE), BF16),
            pltpu.VMEM((VIEWS, VIEW, VIEW), BF16),
            pltpu.VMEM((GROUP, PEERS, VIEW), BF16),
            pltpu.VMEM((COLUMNS, TILE, VIEW), BF16),
            pltpu.VMEM((RB, VIEW), I32),
            pltpu.VMEM((GROUP, VIEW), I32),
            pltpu.VMEM((BANDS, RB, VIEW), BF16),
            pltpu.VMEM((BANDS, GROUP, VIEW), BF16),
            pltpu.VMEM((PEERS, 2, 2 * CAP), F32),
            pltpu.VMEM((PEERS, 2, 2 * CAP), F32),
            pltpu.VMEM((COLUMNS, 1, REGIONS * CAP), F32),
            pltpu.VMEM((ITERS, PEERS, 1, REGIONS * CAP), F32),
            pltpu.VMEM((COLUMNS, BANDS * SLOTS, VIEW), BF16),
            pltpu.VMEM((COLUMNS, BANDS * SLOTS, VIEW), BF16),
            pltpu.VMEM((COLUMNS, SLOTS, VIEW), F32),
            pltpu.VMEM((ITERS, COLUMNS, SLOTS, VIEW), F32),
            pltpu.VMEM((PEERS, 1, 2 * CAP), F32),
            pltpu.VMEM((ITERS, PEERS, 1, 2 * CAP), F32),
            pltpu.VMEM((ITERS, 2, 1, TILE), F32),
            pltpu.VMEM((ITERS, 2, 1, TILE), F32),
            pltpu.VMEM((TILES, TILE), F32),
            pltpu.VMEM((RB, VIEW), F32),
            pltpu.VMEM((COLUMNS, REGIONS * CAP), I32),
            pltpu.VMEM((COLUMNS, REGIONS * CAP), I32),
            pltpu.VMEM((COLUMNS, REGIONS * CAP), F32),
            pltpu.VMEM((COLUMNS, REGIONS * CAP), F32),
            pltpu.VMEM((COLUMNS, REGIONS * CAP), F32),
            pltpu.VMEM((GROUP, VIEW), F32),
            pltpu.VMEM((REGIONS, 2 * CAP, PEERS), BF16),
            pltpu.VMEM((BANDS, KPAD, VIEW), F32),
            pltpu.VMEM((BANDS, VIEWS, VIEW), F32),
            pltpu.VMEM((BANDS, KPAD, VIEW), F32),
            pltpu.VMEM((COLUMNS * SLOTS, KPAD), BF16),
            pltpu.VMEM((CPAD, 2 * TILE), F32),
            pltpu.VMEM((CPAD, TILE), F32),
            pltpu.VMEM((TILES, TILE), F32),
            pltpu.VMEM((8, CPAD), I32),
            pltpu.VMEM((KPAD, BANDS), F32),
            dma((2,)),
            dma((4,)),
            dma((4,)),
            dma((ITERS,)),
            dma((ITERS,)),
            dma((ITERS,)),
            dma((ITERS,)),
            dma((ITERS,)),
            dma((ITERS,)),
            dma((ITERS, 2)),
            dma((ITERS, 2)),
        ],
        compiler_params=pltpu.CompilerParams(
            collective_id=0, has_side_effects=True, vmem_limit_bytes=48 * 1024 * 1024
        ),
    )(
        node_temp.reshape(TILES, TILE),
        node_diag.reshape(TILES, TILE),
        node_source.reshape(TILES, TILE),
        cond_rows.reshape(1, CONDS),
        cond_cols.reshape(1, CONDS),
        view_scales.reshape(VIEWS, BANDS),
        view_rows.reshape(1, VIEWS),
        view_cols.reshape(1, VIEWS),
        band_frac,
        absorb,
        emis,
        patch_dest.reshape(RB, VIEW),
        patch_node,
        cond_blocks.reshape(CONDS, TILE, TILE),
        view_blocks.reshape(VIEWS, VIEW, VIEW),
    )
    return node_final.reshape(TILES * TILE), patch_flux


def solution(mesh):
    placed = (
        P(("region", "blk")),
        P(("region", "blk")),
        P(("region", "blk")),
        P("region", "blk", None, None, None),
        P("region", "blk", None),
        P("region", "blk", None),
        P("region", "blk", None, None, None),
        P("region", "blk", None, None),
        P("region", "blk", None),
        P("region", "blk", None),
        P(("region", "blk"), None, None),
        P(("region", "blk"), None, None),
        P(("region", "blk"), None),
        P(("region", "blk"), None, None),
        P(("region", "blk"), None),
    )
    return jax.shard_map(
        shards,
        mesh=mesh,
        in_specs=placed,
        out_specs=(P(("region", "blk")), P(("region", "blk"), None)),
        check_vma=False,
    )
```

time: 773 us -> 97.5 us (0.13)
  local copies, waits for them, and re-layouts: 254 us -> 10.6 us
  other arithmetic: 224 us -> 0 us
  waiting for transfers between devices: 154 us -> 0 us
  Pallas kernels: 0 us -> 85.6 us
  blocking collectives: 53.1 us -> 0 us
  starting transfers between devices: 38.5 us -> 0 us
  matrix products: 35.4 us -> 0 us
  between operations: 14.7 us -> 0.65 us
    scatter-add x4 -> x0, other arithmetic: 209 us -> none  [the longest x2 105 us: shards(): emis_sum = jax.ops.segment_sum(arrived[1], target, num_segments=node_dev)]
    gather x8 -> x0, local copies, waits for them, and re-layouts: 185 us -> none  [the longest x4 91.2 us: shards(): answer = (node_temps[target] * filled).reshape(peer_count, capacity)]
    reduce_scatter x2 -> x0, waiting for transfers between devices: 120 us -> none  [shards(): lax.psum_scatter(partial_value, 'blk', scatter_dimension=0, tiled=True)]
    pallas_call x0 -> x1, Pallas kernels: none -> 85.6 us  [shards(): pl.pallas_call(kernel, out_shape=(jax.ShapeDtypeStruct((TILES, TILE), F32...]
    scatter x4 -> x0, local copies, waits for them, and re-layouts: 56.6 us -> none  [the longest x2 25.5 us: shards(): jnp.zeros((2, peer_count * capacity), jnp.float32).at[:, send_place]]
    dot_general x12 -> x0, matrix products: 35.4 us -> none  [the longest x2 15.8 us: shards(): jnp.einsum('kij,kbj->kbi', blocks, col_emit, preferred_element_type=jnp.f...]
    all_to_all x2 -> x0, blocking collectives: 34.6 us -> none  [the longest x1 20.8 us: shards(): lax.all_to_all(requests.reshape(peer_count, capacity), ('region', 'blk'),...]
    all_to_all x3 -> x0, waiting for transfers between devices: 28.1 us -> none  [the longest x2 18.7 us: relay_out(): lax.all_to_all(outgoing, ('region', 'blk'), split_axis=1, concat_axis=1,...]
  transfers between devices with their start and end apart: 9 -> 0, of which waited for: 7 -> 0; matrix products, arithmetic and copies ran while one was open for 2% -> 0% of each run, Pallas kernels for 0% -> 0%
where the time goes in v1:
time: 97.5 us; the launch traced here: 96.8 us
  Pallas kernels  85.6 us (88%)
  local copies, waits for them, and re-layouts  10.6 us (11%)
    pallas_call x1, Pallas kernels, shards(): pl.pallas_call(kernel, out_shape=(jax.ShapeDtypeStruct((TILES, TILE), F32...  85.6 us
    unnamed x26, local copies, waits for them, and re-layouts  10.6 us

profile of v1, /device:TPU:1, one launch (start us, length us, event | category | flops | bytes accessed | tf_op | source)
XLA Modules:
  0.0 96.8 jit_solution(4834296045967383792)
XLA Ops:
  0.6 0.7 copy.20
  1.3 0.8 copy.17
  2.1 0.0 copy-start
  2.1 0.8 copy-done
  2.9 0.0 copy-start.1
  2.9 0.8 copy-done.1
  3.6 0.0 copy-start.2
  3.6 0.8 copy-done.2
  4.4 0.0 copy-start.3
  4.4 0.8 copy-done.3
  5.2 0.0 copy-start.4
  5.2 0.8 copy-done.4
  5.9 0.0 copy-start.5
  5.9 0.7 copy-done.5
  6.6 0.0 copy-start.6
  6.6 0.7 copy-done.6
  7.3 0.0 copy-start.7
  7.3 0.7 copy-done.7
  8.0 0.7 copy-done.8
  8.7 0.7 copy-done.9
  9.4 0.7 copy-done.10
  10.0 85.6 %shard_map.158 = (f32[64,128]{1,0:T(8,128)S(1)}, f32[16,256]{1,0:T(8,128)S(1)}) custom-call(f32[64,128]{1,0:T(8,128)S(1)} %bitcast.16, f32[64,128]{1,0:T(8,128)S(1)} %bitcast.17, f32[64,128]{1,0:T(8,128)S(1)} %bitcast.18, s32[1,192]{1,0:T(1,128)S(1)} %bitcast.20, s32[1,192]{1,0:T(1,128)S(1)} %bitcast.21, f32[96,4]{1,0:T(8,128)S(1)} %bitcast.14, ...), custom_call_target="tpu_custom_call" | custom-call | tf_op jit(solution)/shard_map/pallas_call | solution.py:527
  95.6 0.6 copy.23
  96.2 0.6 copy.24
  (3 shorter events, 0.0 us)
Async XLA Ops:
  2.1 0.8 copy-start
  2.9 0.8 copy-start.1
  3.6 0.8 copy-start.2
  4.4 0.8 copy-start.3
  5.2 0.8 copy-start.4
  5.9 0.7 copy-start.5
  6.6 0.7 copy-start.6
  7.3 0.7 copy-start.7
  8.0 0.7 copy-start.8
  8.7 0.7 copy-start.9
  9.4 0.7 copy-start.10

commit v2 on v1

--- a/solution.py
+++ b/solution.py
@@ -29,6 +29,15 @@
 I32 = jnp.int32
 
 
+FAR_GROUPS = [
+    rx * 32 + z * 8
+    for rx, z in sorted(
+        ((rx, z) for rx in range(4) for z in range(4)),
+        key=lambda g: -((0, 1, 2, 1)[g[0]] + (0, 1, 2, 1)[g[1]]),
+    )
+]
+
+
 def mm(a, b):
     return jnp.dot(a, b, preferred_element_type=F32)
 
@@ -69,23 +78,36 @@
 
 
 def kernel(
-    temp_ref,
-    diag_ref,
-    source_ref,
-    crow_ref,
-    ccol_ref,
-    scale_ref,
-    vrow_ref,
-    vcol_ref,
-    frac_ref,
-    absorb_ref,
-    emis_ref,
-    dest_ref,
-    node_ref,
+    dest_hbm,
+    node_hbm,
+    emis_hbm,
+    temp_hbm,
+    vrow_hbm,
+    vcol_hbm,
+    frac_hbm,
+    crow_hbm,
+    ccol_hbm,
+    scale_hbm,
+    absorb_hbm,
+    diag_hbm,
+    source_hbm,
     cond_hbm,
     view_hbm,
     node_out,
     flux_out,
+    dest_ref,
+    node_ref,
+    emis_ref,
+    temps,
+    vrow_ref,
+    vcol_ref,
+    frac_ref,
+    crow_ref,
+    ccol_ref,
+    scale_ref,
+    absorb_ref,
+    diag_ref,
+    source_ref,
     cb,
     vb,
     ohd,
@@ -106,7 +128,6 @@
     f_recv,
     halo_send,
     halo_recv,
-    temps,
     emf,
     hi4,
     lo4,
@@ -125,6 +146,7 @@
     pads,
     scalep,
     load_sem,
+    small_sem,
     setup_send,
     setup_recv,
     ans_ssem,
@@ -144,6 +166,19 @@
         p = jnp.bitwise_xor(me, i)
         return p, (lax.shift_right_logical(p, 5), jnp.bitwise_and(p, COLUMNS - 1))
 
+    def all_peers(step):
+        for base in FAR_GROUPS:
+            if base:
+                lax.fori_loop(0, 8, lambda w, z: (step(base + jnp.bitwise_xor(w, 4)), z)[1], 0)
+            else:
+                for w in (0, 1, 2, 3, 5, 6, 7):
+                    step(w ^ 4)
+
+    def column_peers(step):
+        far = 20
+        lax.fori_loop(0, far, lambda w, z: (step(jnp.bitwise_xor(w, far)), z)[1], 0)
+        lax.fori_loop(far + 1, COLUMNS, lambda w, z: (step(jnp.bitwise_xor(w, far)), z)[1], 0)
+
     def push(src, dst, ssem, rsem, where):
         pltpu.make_async_remote_copy(
             src_ref=src,
@@ -157,20 +192,41 @@
     def drain(ref, sem):
         pltpu.make_async_copy(ref, ref, sem).wait()
 
+    barrier = pltpu.get_barrier_semaphore()
+
+    def greet(i):
+        pl.semaphore_signal(barrier, inc=1, device_id=peer(i)[1], device_id_type=MESH)
+
+    all_peers(greet)
+
     cond_load = pltpu.make_async_copy(cond_hbm, cb, load_sem.at[0])
     view_load = pltpu.make_async_copy(view_hbm, vb, load_sem.at[1])
+    pairs = [
+        (dest_hbm, dest_ref),
+        (node_hbm, node_ref),
+        (emis_hbm, emis_ref),
+        (temp_hbm, temps),
+        (vrow_hbm, vrow_ref),
+        (vcol_hbm, vcol_ref),
+        (frac_hbm, frac_ref),
+        (crow_hbm, crow_ref),
+        (ccol_hbm, ccol_ref),
+        (scale_hbm, scale_ref),
+        (absorb_hbm, absorb_ref),
+        (diag_hbm, diag_ref),
+        (source_hbm, source_ref),
+    ]
+    small = [
+        pltpu.make_async_copy(src, dst, small_sem.at[n]) for n, (src, dst) in enumerate(pairs)
+    ]
+    for load in small:
+        load.start()
     cond_load.start()
     view_load.start()
 
-    barrier = pltpu.get_barrier_semaphore()
-
-    def greet(i, carry):
-        pl.semaphore_signal(barrier, inc=1, device_id=peer(i)[1], device_id_type=MESH)
-        return carry
-
-    lax.fori_loop(1, PEERS, greet, 0)
-
-    temps[...] = temp_ref[...]
+    for load in small:
+        load.wait()
+
     emf[...] = emis_ref[...].astype(F32)
     upper_tri = pick(iota((VIEW, VIEW), 0) < iota((VIEW, VIEW), 1))
     peer_row = iota((PEERS, VIEW), 0)
@@ -180,13 +236,14 @@
 
     def route(u, carry):
         count, first, second = carry
-        dest = dest_ref[pl.ds(u, 1), :]
+        dest = dest_ref[u]
         node = node_ref[pl.ds(u, 1), :]
         hit = jnp.where(peer_row == dest, 1.0, 0.0)
         hit16 = hit.astype(BF16)
         before = mm(hit16, upper_tri)
         rank = jnp.sum(hit * (before + count), axis=0, keepdims=True).astype(I32)
         code_mine[pl.ds(u, 1), :] = dest * CAP + rank
+        ohd[r * RB + u] = hit16
         high = (lax.shift_right_logical(node, 7) + 1).astype(F32)
         low = jnp.bitwise_and(node, TILE - 1).astype(F32)
         match = slot_rank == rank
@@ -236,8 +293,8 @@
     for b in range(BANDS):
         frac_mine[b] = frac_ref[:, b, :]
     ohcol = pick(iota((GROUP, KPAD), 0) == vcol)
-    scalep[...] = jnp.zeros((KPAD, BANDS), F32)
-    scalep[0:VIEWS, :] = scale_ref[...]
+    scalep[...] = jnp.zeros((8, KPAD), F32)
+    scalep[0:BANDS, 0:VIEWS] = scale_ref[...]
     terms[...] = jnp.zeros((CPAD, TILE), F32)
     oh_ctile = pick(iota((TILES, CPAD), 0) == crow)
     ccol_at = jnp.where(ccol == 0, TILES, jnp.where(ccol == TILES + 1, TILES + 1, ccol - 1))
@@ -245,18 +302,16 @@
 
     pl.semaphore_wait(barrier, PEERS - 1)
 
-    def send_request(i, carry):
+    mine = pl.ds(pl.multiple_of(r * RB, RB), RB)
+    def send_request(i):
         p, where = peer(i)
         push(req_send.at[p], req_recv.at[me], setup_send.at[0], setup_recv.at[0], where)
-        return carry
-
-    lax.fori_loop(1, PEERS, send_request, 0)
-    req_recv[pl.ds(me, 1)] = req_send[pl.ds(me, 1)]
-    mine = pl.ds(pl.multiple_of(r * RB, RB), RB)
+
+    all_peers(send_request)
     for i in range(1, REGIONS):
         where = (jnp.bitwise_xor(r, i), c)
         push(code_mine, code_all.at[mine], setup_send.at[1], setup_recv.at[1], where)
-        push(frac_mine, frac_all.at[:, mine, :], setup_send.at[2], setup_recv.at[2], where)
+    req_recv[pl.ds(me, 1)] = req_send[pl.ds(me, 1)]
     code_all[mine, :] = code_mine[...]
     frac_all[:, mine, :] = frac_mine[...]
 
@@ -282,18 +337,13 @@
 
     send_halo(0)
 
-    others = pl.ds(0, (REGIONS - 1) * RB)
-    drain(code_all.at[others], setup_recv.at[1])
-    drain(code_all.at[others], setup_send.at[1])
-
-    def build_dest(q, carry):
-        ohd[q] = pick(peer_row == lax.shift_right_logical(code_all[pl.ds(q, 1), :], 6))
+    view_load.wait()
+
+    def turn(k, carry):
+        vb[k] = vb[k].T
         return carry
 
-    lax.fori_loop(0, GROUP, build_dest, 0, unroll=4)
-    drain(frac_all.at[:, others, :], setup_recv.at[2])
-    drain(frac_all.at[:, others, :], setup_send.at[2])
-
+    lax.fori_loop(0, VIEWS, turn, 0, unroll=4)
     drain(req_recv.at[0 : PEERS - 1], setup_recv.at[0])
     drain(req_recv.at[0 : PEERS - 1], setup_send.at[0])
     asked = req_recv[:, 0, :]
@@ -322,14 +372,13 @@
             )
             return carry
 
-        lax.fori_loop(0, COLUMNS, look, 0, unroll=8)
-
-        def send(i, carry):
-            p, where = peer(i)
+        lax.fori_loop(0, COLUMNS, look, 0, unroll=16)
+
+        def send(i):
+            where = peer(i)[1]
             push(ans_send.at[where[1]], ans_recv.at[it, me], ans_ssem.at[it], ans_rsem.at[it], where)
-            return carry
-
-        lax.fori_loop(1, PEERS, send, 0)
+
+        all_peers(send)
         ans_recv[it, pl.ds(me, 1)] = ans_send[pl.ds(c, 1)]
 
     def conduct(it):
@@ -357,6 +406,19 @@
         return mm(oh_ctile, up) + mm(oh_ctile, down)
 
     answer(0)
+    for i in range(1, REGIONS):
+        where = (jnp.bitwise_xor(r, i), c)
+        push(frac_mine, frac_all.at[:, mine, :], setup_send.at[2], setup_recv.at[2], where)
+    others = pl.ds(0, (REGIONS - 1) * RB)
+    drain(code_all.at[others], setup_recv.at[1])
+    drain(code_all.at[others], setup_send.at[1])
+
+    def build_dest(n, carry):
+        q = lax.rem(n + (r + 1) * RB, GROUP)
+        ohd[q] = pick(peer_row == lax.shift_right_logical(code_all[pl.ds(q, 1), :], 6))
+        return carry
+
+    lax.fori_loop(0, GROUP - RB, build_dest, 0, unroll=8)
 
     codes = req_recv[pl.ds(r * COLUMNS, COLUMNS), 1, :]
     row_codes = jnp.concatenate(
@@ -373,20 +435,20 @@
         ]
         ab_send[:, b * SLOTS : (b + 2) * SLOTS, :] = jnp.concatenate(pair, axis=1).astype(BF16)
 
-    def send_absorb(i, carry):
-        p = jnp.bitwise_xor(c, i)
-        push(ab_send.at[p], ab_recv.at[c], setup_send.at[3], setup_recv.at[3], (r, p))
-        return carry
-
-    lax.fori_loop(1, COLUMNS, send_absorb, 0)
-    ab_recv[pl.ds(c, 1)] = ab_send[pl.ds(c, 1)]
-
     def gather_emis(j, acc):
         spread = jnp.where(tile_row == hi4[pl.ds(j, 1), :], em4[pl.ds(j, 1), :], 0.0)
         return acc + mm_nt(spread.astype(BF16), ohlo[j])
 
     esum[...] = lax.fori_loop(0, COLUMNS, gather_emis, jnp.zeros((TILES, TILE), F32), unroll=4)
 
+    def send_absorb(i):
+        p = jnp.bitwise_xor(c, i)
+        push(ab_send.at[p], ab_recv.at[c], setup_send.at[3], setup_recv.at[3], (r, p))
+
+    column_peers(send_absorb)
+    ab_recv[pl.ds(c, 1)] = ab_send[pl.ds(c, 1)]
+    drain(frac_all.at[:, others, :], setup_recv.at[2])
+    drain(frac_all.at[:, others, :], setup_send.at[2])
     rank_row = iota((CAP, VIEW), 0)
 
     for it in range(ITERS):
@@ -408,26 +470,27 @@
             patchq[pl.ds(q, 1), :] = squared * squared
             return carry
 
-        lax.fori_loop(0, GROUP, unpack, 0, unroll=8)
+        lax.fori_loop(0, GROUP, unpack, 0, unroll=32)
         quartic = patchq[...]
         for b in range(BANDS):
             emit = (frac_all[b].astype(F32) * quartic).astype(BF16)
             ecol[b] = mm_tn(ohcol, emit)
-        if it == 0:
-            view_load.wait()
-
         def view(k, carry):
-            prod[:, k, :] = mm_nt(ecol[:, k, :].astype(BF16), vb[k])
+            prod[:, k, :] = mm(ecol[:, k, :].astype(BF16), vb[k])
             return carry
 
-        lax.fori_loop(0, VIEWS, view, 0, unroll=8)
+        lax.fori_loop(0, VIEWS, view, 0, unroll=32)
         if it == 0:
             drain(ab_recv.at[0 : COLUMNS - 1], setup_recv.at[3])
             drain(ab_recv.at[0 : COLUMNS - 1], setup_send.at[3])
             rows = ab_recv[...].astype(F32)
+            diagonal = iota((KPAD, KPAD), 0) == iota((KPAD, KPAD), 1)
             for b in range(BANDS):
                 mine_b = rows[:, b * SLOTS : (b + 1) * SLOTS, :].reshape(COLUMNS * SLOTS, VIEW)
-                abk[b] = mm_tn(ohslot[...], mine_b.astype(BF16)) * scalep[:, b : b + 1]
+                column = jnp.sum(
+                    jnp.where(diagonal, scalep[b : b + 1, :], 0.0), axis=1, keepdims=True
+                )
+                abk[b] = mm_tn(ohslot[...], mine_b.astype(BF16)) * column
         gained = prod[0] * abk[0, 0:VIEWS]
         for b in range(1, BANDS):
             gained = gained + prod[b] * abk[b, 0:VIEWS]
@@ -436,12 +499,11 @@
         )
         g_send[...] = (mm(ohslot[...], up) + mm(ohslot[...], down)).reshape(COLUMNS, SLOTS, VIEW)
 
-        def send_rows(i, carry):
+        def send_rows(i):
             p = jnp.bitwise_xor(c, i)
             push(g_send.at[p], g_recv.at[it, c], g_ssem.at[it], g_rsem.at[it], (r, p))
-            return carry
-
-        lax.fori_loop(1, COLUMNS, send_rows, 0)
+
+        column_peers(send_rows)
         g_recv[it, pl.ds(c, 1)] = g_send[pl.ds(c, 1)]
         if it == 0:
             cond_load.wait()
@@ -454,20 +516,23 @@
         up, down = halves(flux)
         up, down = up.astype(F32), down.astype(F32)
         packed = jnp.zeros((PEERS, 2 * CAP), F32)
-        for u in range(RB):
-            rank = jnp.bitwise_and(code_mine[u : u + 1, :], CAP - 1)
-            spread = jnp.where(
-                slot_rank == rank, jnp.where(slot_low, up[u : u + 1], down[u : u + 1]), 0.0
-            )
-            packed = packed + mm_nt(ohd[r * RB + u], spread.astype(BF16))
+        for first_row in range(0, RB, 8):
+            left, right = [], []
+            for u in range(first_row, first_row + 8):
+                rank = jnp.bitwise_and(code_mine[u : u + 1, :], CAP - 1)
+                spread = jnp.where(
+                    slot_rank == rank, jnp.where(slot_low, up[u : u + 1], down[u : u + 1]), 0.0
+                )
+                left.append(ohd[r * RB + u])
+                right.append(spread.astype(BF16))
+            packed = packed + mm_nt(jnp.concatenate(left, axis=1), jnp.concatenate(right, axis=1))
         f_send[:, 0, :] = packed
 
-        def send_flux(i, carry):
+        def send_flux(i):
             p, where = peer(i)
             push(f_send.at[p], f_recv.at[it, me], f_ssem.at[it], f_rsem.at[it], where)
-            return carry
-
-        lax.fori_loop(1, PEERS, send_flux, 0)
+
+        all_peers(send_flux)
         f_recv[it, pl.ds(me, 1)] = f_send[pl.ds(me, 1)]
         drain(f_recv.at[it, 0 : PEERS - 1], f_rsem.at[it])
         drain(f_recv.at[it, 0 : PEERS - 1], f_ssem.at[it])
@@ -475,20 +540,16 @@
         fh4[...] = rows_to_slots(came, False)
         fl4[...] = rows_to_slots(came, True)
 
-        def gather_heat(j, acc):
-            hit = tile_row == hi4[pl.ds(j, 1), :]
-            spread = jnp.concatenate(
-                [
-                    jnp.where(hit, fh4[pl.ds(j, 1), :], 0.0).astype(BF16),
-                    jnp.where(hit, fl4[pl.ds(j, 1), :], 0.0).astype(BF16),
-                ],
-                axis=0,
-            )
-            return acc + mm_nt(spread, ohlo[j])
-
-        heat = lax.fori_loop(
-            0, COLUMNS, gather_heat, jnp.zeros((2 * TILES, TILE), F32), unroll=4
-        )
+        heat = jnp.zeros((2 * TILES, TILE), F32)
+        for j in range(0, COLUMNS, 8):
+            left, right = [], []
+            for n in range(j, j + 8):
+                hit = tile_row == hi4[n : n + 1, :]
+                up = jnp.where(hit, fh4[n : n + 1, :], 0.0).astype(BF16)
+                down = jnp.where(hit, fl4[n : n + 1, :], 0.0).astype(BF16)
+                left.append(jnp.concatenate([up, down], axis=0))
+                right.append(ohlo[n])
+            heat = heat + mm_nt(jnp.concatenate(left, axis=1), jnp.concatenate(right, axis=1))
         old = temps[...]
         residual = (
             diag_ref[...] * old - conducted - (heat[0:TILES] + heat[TILES:]) - source_ref[...]
@@ -522,7 +583,7 @@
     patch_node,
 ):
     vmem = pl.BlockSpec(memory_space=pltpu.VMEM)
-    hbm = pl.BlockSpec(memory_space=pl.ANY)
+    hbm = pl.BlockSpec(memory_space=pltpu.HBM)
     dma = pltpu.SemaphoreType.DMA
     node_final, patch_flux = pl.pallas_call(
         kernel,
@@ -530,9 +591,22 @@
             jax.ShapeDtypeStruct((TILES, TILE), F32),
             jax.ShapeDtypeStruct((RB, VIEW), F32),
         ),
-        in_specs=[vmem] * 13 + [hbm] * 2,
+        in_specs=[hbm] * 15,
         out_specs=(vmem, vmem),
         scratch_shapes=[
+            pltpu.VMEM((RB, 1, VIEW), I32),
+            pltpu.VMEM((RB, VIEW), I32),
+            pltpu.VMEM((RB, VIEW), BF16),
+            pltpu.VMEM((TILES, TILE), F32),
+            pltpu.VMEM((1, VIEWS), I32),
+            pltpu.VMEM((1, VIEWS), I32),
+            pltpu.VMEM((RB, BANDS, VIEW), BF16),
+            pltpu.VMEM((1, CONDS), I32),
+            pltpu.VMEM((1, CONDS), I32),
+            pltpu.VMEM((BANDS, VIEWS), F32),
+            pltpu.VMEM((RB, BANDS, VIEW), BF16),
+            pltpu.VMEM((TILES, TILE), F32),
+            pltpu.VMEM((TILES, TILE), F32),
             pltpu.VMEM((CONDS, TILE, TILE), BF16),
             pltpu.VMEM((VIEWS, VIEW, VIEW), BF16),
             pltpu.VMEM((GROUP, PEERS, VIEW), BF16),
@@ -553,7 +627,6 @@
             pltpu.VMEM((ITERS, PEERS, 1, 2 * CAP), F32),
             pltpu.VMEM((ITERS, 2, 1, TILE), F32),
             pltpu.VMEM((ITERS, 2, 1, TILE), F32),
-            pltpu.VMEM((TILES, TILE), F32),
             pltpu.VMEM((RB, VIEW), F32),
             pltpu.VMEM((COLUMNS, REGIONS * CAP), I32),
             pltpu.VMEM((COLUMNS, REGIONS * CAP), I32),
@@ -570,8 +643,9 @@
             pltpu.VMEM((CPAD, TILE), F32),
             pltpu.VMEM((TILES, TILE), F32),
             pltpu.VMEM((8, CPAD), I32),
-            pltpu.VMEM((KPAD, BANDS), F32),
+            pltpu.VMEM((8, KPAD), F32),
             dma((2,)),
+            dma((13,)),
             dma((4,)),
             dma((4,)),
             dma((ITERS,)),
@@ -584,22 +658,22 @@
             dma((ITERS, 2)),
         ],
         compiler_params=pltpu.CompilerParams(
-            collective_id=0, has_side_effects=True, vmem_limit_bytes=48 * 1024 * 1024
+            collective_id=0, has_side_effects=True, vmem_limit_bytes=64 * 1024 * 1024
         ),
     )(
+        patch_dest.reshape(RB, 1, VIEW),
+        patch_node,
+        emis,
         node_temp.reshape(TILES, TILE),
-        node_diag.reshape(TILES, TILE),
-        node_source.reshape(TILES, TILE),
-        cond_rows.reshape(1, CONDS),
-        cond_cols.reshape(1, CONDS),
-        view_scales.reshape(VIEWS, BANDS),
         view_rows.reshape(1, VIEWS),
         view_cols.reshape(1, VIEWS),
         band_frac,
+        cond_rows.reshape(1, CONDS),
+        cond_cols.reshape(1, CONDS),
+        view_scales.reshape(VIEWS, BANDS).T,
         absorb,
-        emis,
-        patch_dest.reshape(RB, VIEW),
-        patch_node,
+        node_diag.reshape(TILES, TILE),
+        node_source.reshape(TILES, TILE),
         cond_blocks.reshape(CONDS, TILE, TILE),
         view_blocks.reshape(VIEWS, VIEW, VIEW),
     )

time: 97.5 us -> 83.1 us (0.85)
  local copies, waits for them, and re-layouts: 10.6 us -> 2.7 us
  Pallas kernels: 85.6 us -> 79.5 us
    unnamed x26 -> x2, local copies, waits for them, and re-layouts: 10.6 us -> 2.7 us
    pallas_call x1, Pallas kernels: 85.6 us -> 79.5 us  [shards(): pl.pallas_call(kernel, out_shape=(jax.ShapeDtypeStruct((TILES, TILE), F32...]
where the time goes in v2:
time: 83.1 us; the launch traced here: 82.8 us
  Pallas kernels  79.5 us (96%)
  local copies, waits for them, and re-layouts  2.7 us (3%)
    pallas_call x1, Pallas kernels, shards(): pl.pallas_call(kernel, out_shape=(jax.ShapeDtypeStruct((TILES, TILE), F32...  79.5 us
    unnamed x2, local copies, waits for them, and re-layouts  2.7 us

profile of v2, /device:TPU:1, one launch (start us, length us, event | category | flops | bytes accessed | tf_op | source)
XLA Modules:
  0.0 82.8 jit_solution(13100175189018428803)
XLA Ops:
  0.6 79.5 %shard_map.158 = (f32[64,128]{1,0:T(8,128)}, f32[16,256]{1,0:T(8,128)}) custom-call(s32[16,1,256]{2,1,0:T(1,128)} %bitcast.20, s32[16,256]{1,0:T(8,128)} %node_hbm.1, bf16[16,256]{1,0:T(8,128)(2,1)} %emis_hbm.1, f32[64,128]{1,0:T(8,128)} %bitcast.16, s32[1,96]{1,0:T(1,128)} %bitcast.24, s32[1,96]{1,0:T(1,128)} %bitcast.25, bf16[16,4,256]{2,1,0:T(4,128)(2,1)} %frac_hbm.1, ...), custom_call_target="tpu_custom_call" | custom-call | tf_op jit(solution)/shard_map/pallas_call | solution.py:588
  80.1 1.4 %copy.19 = f32[8192]{0:T(1024)} copy(f32[8192]{0:T(1024)} %bitcast.19) | data formatting | bytes 65536
  81.5 1.3 %copy.20 = f32[16,256]{1,0:T(8,128)} copy(f32[16,256]{1,0:T(8,128)} %get-tuple-element.9) | data formatting | bytes 32768

commit v3 on v2

--- a/solution.py
+++ b/solution.py
@@ -23,6 +23,7 @@
 TILE = 128
 CONDS = 192
 CPAD = 256
+TURNED = 56
 MESH = pl.DeviceIdType.MESH
 F32 = jnp.float32
 BF16 = jnp.bfloat16
@@ -292,7 +293,7 @@
 
     for b in range(BANDS):
         frac_mine[b] = frac_ref[:, b, :]
-    ohcol = pick(iota((GROUP, KPAD), 0) == vcol)
+    ohcol = jnp.where(iota((KPAD, KPAD), 0) == vcol, 1.0, 0.0).T[:, 0:GROUP].astype(BF16)
     scalep[...] = jnp.zeros((8, KPAD), F32)
     scalep[0:BANDS, 0:VIEWS] = scale_ref[...]
     terms[...] = jnp.zeros((CPAD, TILE), F32)
@@ -343,7 +344,7 @@
         vb[k] = vb[k].T
         return carry
 
-    lax.fori_loop(0, VIEWS, turn, 0, unroll=4)
+    lax.fori_loop(0, TURNED, turn, 0, unroll=4)
     drain(req_recv.at[0 : PEERS - 1], setup_recv.at[0])
     drain(req_recv.at[0 : PEERS - 1], setup_send.at[0])
     asked = req_recv[:, 0, :]
@@ -354,18 +355,17 @@
     tile_row = iota((TILES, VIEW), 0)
     node_row = iota((TILE, VIEW), 0)
 
-    def build_node(j, carry):
-        ohlo[j] = pick(node_row == lo4[pl.ds(j, 1), :])
-        return carry
-
-    lax.fori_loop(0, COLUMNS, build_node, 0, unroll=4)
-
     def answer(it):
         up, down = halves(temps[...])
         both = jnp.concatenate([up, down], axis=0)
 
         def look(j, carry):
-            found = mm(both, ohlo[j])
+            if it == 0:
+                hot = pick(node_row == lo4[pl.ds(j, 1), :])
+                ohlo[j] = hot
+            else:
+                hot = ohlo[j]
+            found = mm(both, hot)
             found = found[0:TILES] + found[TILES:]
             ans_send[j] = jnp.sum(
                 jnp.where(tile_row == hi4[pl.ds(j, 1), :], found, 0.0), axis=0, keepdims=True
@@ -435,18 +435,13 @@
         ]
         ab_send[:, b * SLOTS : (b + 2) * SLOTS, :] = jnp.concatenate(pair, axis=1).astype(BF16)
 
-    def gather_emis(j, acc):
-        spread = jnp.where(tile_row == hi4[pl.ds(j, 1), :], em4[pl.ds(j, 1), :], 0.0)
-        return acc + mm_nt(spread.astype(BF16), ohlo[j])
-
-    esum[...] = lax.fori_loop(0, COLUMNS, gather_emis, jnp.zeros((TILES, TILE), F32), unroll=4)
-
     def send_absorb(i):
         p = jnp.bitwise_xor(c, i)
         push(ab_send.at[p], ab_recv.at[c], setup_send.at[3], setup_recv.at[3], (r, p))
 
     column_peers(send_absorb)
     ab_recv[pl.ds(c, 1)] = ab_send[pl.ds(c, 1)]
+    lax.fori_loop(TURNED, VIEWS, turn, 0, unroll=4)
     drain(frac_all.at[:, others, :], setup_recv.at[2])
     drain(frac_all.at[:, others, :], setup_send.at[2])
     rank_row = iota((CAP, VIEW), 0)
@@ -474,7 +469,7 @@
         quartic = patchq[...]
         for b in range(BANDS):
             emit = (frac_all[b].astype(F32) * quartic).astype(BF16)
-            ecol[b] = mm_tn(ohcol, emit)
+            ecol[b] = mm(ohcol, emit)
         def view(k, carry):
             prod[:, k, :] = mm(ecol[:, k, :].astype(BF16), vb[k])
             return carry
@@ -534,6 +529,18 @@
 
         all_peers(send_flux)
         f_recv[it, pl.ds(me, 1)] = f_send[pl.ds(me, 1)]
+        if it == 0:
+            weight = jnp.zeros((TILES, TILE), F32)
+            for j in range(0, COLUMNS, 8):
+                left, right = [], []
+                for n in range(j, j + 8):
+                    hit = tile_row == hi4[n : n + 1, :]
+                    left.append(jnp.where(hit, em4[n : n + 1, :], 0.0).astype(BF16))
+                    right.append(ohlo[n])
+                weight = weight + mm_nt(
+                    jnp.concatenate(left, axis=1), jnp.concatenate(right, axis=1)
+                )
+            esum[...] = weight
         drain(f_recv.at[it, 0 : PEERS - 1], f_rsem.at[it])
         drain(f_recv.at[it, 0 : PEERS - 1], f_ssem.at[it])
         came = f_recv[it, :, 0, :]

time: 83.1 us -> 81.4 us (0.980)
  Pallas kernels: 79.5 us -> 77.8 us
    pallas_call x1, Pallas kernels: 79.5 us -> 77.8 us  [shards(): pl.pallas_call(kernel, out_shape=(jax.ShapeDtypeStruct((TILES, TILE), F32...]
where the time goes in v3:
time: 81.4 us; the launch traced here: 81.1 us
  Pallas kernels  77.8 us (96%)
  local copies, waits for them, and re-layouts  2.7 us (3%)
    pallas_call x1, Pallas kernels, shards(): pl.pallas_call(kernel, out_shape=(jax.ShapeDtypeStruct((TILES, TILE), F32...  77.8 us
    unnamed x2, local copies, waits for them, and re-layouts  2.7 us

profile of v3, /device:TPU:1, one launch (start us, length us, event | category | flops | bytes accessed | tf_op | source)
XLA Modules:
  0.0 81.1 jit_solution(1726940896819172202)
XLA Ops:
  0.6 77.8 %shard_map.158 = (f32[64,128]{1,0:T(8,128)}, f32[16,256]{1,0:T(8,128)}) custom-call(s32[16,1,256]{2,1,0:T(1,128)} %bitcast.20, s32[16,256]{1,0:T(8,128)} %node_hbm.1, bf16[16,256]{1,0:T(8,128)(2,1)} %emis_hbm.1, f32[64,128]{1,0:T(8,128)} %bitcast.16, s32[1,96]{1,0:T(1,128)} %bitcast.24, s32[1,96]{1,0:T(1,128)} %bitcast.25, bf16[16,4,256]{2,1,0:T(4,128)(2,1)} %frac_hbm.1, ...), custom_call_target="tpu_custom_call" | custom-call | tf_op jit(solution)/shard_map/pallas_call | solution.py:595
  78.4 1.4 %copy.19 = f32[8192]{0:T(1024)} copy(f32[8192]{0:T(1024)} %bitcast.19) | data formatting | bytes 65536
  79.8 1.3 %copy.20 = f32[16,256]{1,0:T(8,128)} copy(f32[16,256]{1,0:T(8,128)} %get-tuple-element.9) | data formatting | bytes 32768

commit v4 on v3

--- a/solution.py
+++ b/solution.py
@@ -24,6 +24,7 @@
 CONDS = 192
 CPAD = 256
 TURNED = 56
+LATE = 72
 MESH = pl.DeviceIdType.MESH
 F32 = jnp.float32
 BF16 = jnp.bfloat16
@@ -409,17 +410,6 @@
     for i in range(1, REGIONS):
         where = (jnp.bitwise_xor(r, i), c)
         push(frac_mine, frac_all.at[:, mine, :], setup_send.at[2], setup_recv.at[2], where)
-    others = pl.ds(0, (REGIONS - 1) * RB)
-    drain(code_all.at[others], setup_recv.at[1])
-    drain(code_all.at[others], setup_send.at[1])
-
-    def build_dest(n, carry):
-        q = lax.rem(n + (r + 1) * RB, GROUP)
-        ohd[q] = pick(peer_row == lax.shift_right_logical(code_all[pl.ds(q, 1), :], 6))
-        return carry
-
-    lax.fori_loop(0, GROUP - RB, build_dest, 0, unroll=8)
-
     codes = req_recv[pl.ds(r * COLUMNS, COLUMNS), 1, :]
     row_codes = jnp.concatenate(
         [
@@ -441,7 +431,18 @@
 
     column_peers(send_absorb)
     ab_recv[pl.ds(c, 1)] = ab_send[pl.ds(c, 1)]
-    lax.fori_loop(TURNED, VIEWS, turn, 0, unroll=4)
+    others = pl.ds(0, (REGIONS - 1) * RB)
+    drain(code_all.at[others], setup_recv.at[1])
+    drain(code_all.at[others], setup_send.at[1])
+
+    def build_dest(n, carry):
+        q = lax.rem(n + (r + 1) * RB, GROUP)
+        ohd[q] = pick(peer_row == lax.shift_right_logical(code_all[pl.ds(q, 1), :], 6))
+        return carry
+
+    lax.fori_loop(0, GROUP - RB, build_dest, 0, unroll=8)
+
+    lax.fori_loop(TURNED, LATE, turn, 0, unroll=4)
     drain(frac_all.at[:, others, :], setup_recv.at[2])
     drain(frac_all.at[:, others, :], setup_send.at[2])
     rank_row = iota((CAP, VIEW), 0)
@@ -474,7 +475,15 @@
             prod[:, k, :] = mm(ecol[:, k, :].astype(BF16), vb[k])
             return carry
 
-        lax.fori_loop(0, VIEWS, view, 0, unroll=32)
+        def view_unturned(k, carry):
+            prod[:, k, :] = mm_nt(ecol[:, k, :].astype(BF16), vb[k])
+            return carry
+
+        if it == 0:
+            lax.fori_loop(0, LATE, view, 0, unroll=36)
+            lax.fori_loop(LATE, VIEWS, view_unturned, 0, unroll=24)
+        else:
+            lax.fori_loop(0, VIEWS, view, 0, unroll=32)
         if it == 0:
             drain(ab_recv.at[0 : COLUMNS - 1], setup_recv.at[3])
             drain(ab_recv.at[0 : COLUMNS - 1], setup_send.at[3])
@@ -541,6 +550,7 @@
                     jnp.concatenate(left, axis=1), jnp.concatenate(right, axis=1)
                 )
             esum[...] = weight
+            lax.fori_loop(LATE, VIEWS, turn, 0, unroll=4)
         drain(f_recv.at[it, 0 : PEERS - 1], f_rsem.at[it])
         drain(f_recv.at[it, 0 : PEERS - 1], f_ssem.at[it])
         came = f_recv[it, :, 0, :]

time: 81.4 us -> 82 us (level)
  no operation moved by 1% of the time
where the time goes in v4:
time: 82 us; the launch traced here: 81.7 us
  Pallas kernels  78.4 us (96%)
  local copies, waits for them, and re-layouts  2.7 us (3%)
    pallas_call x1, Pallas kernels, shards(): pl.pallas_call(kernel, out_shape=(jax.ShapeDtypeStruct((TILES, TILE), F32...  78.4 us
    unnamed x2, local copies, waits for them, and re-layouts  2.7 us

profile of v4, /device:TPU:1, one launch (start us, length us, event | category | flops | bytes accessed | tf_op | source)
XLA Modules:
  0.0 81.7 jit_solution(15662228355176951666)
XLA Ops:
  0.6 78.4 %shard_map.158 = (f32[64,128]{1,0:T(8,128)}, f32[16,256]{1,0:T(8,128)}) custom-call(s32[16,1,256]{2,1,0:T(1,128)} %bitcast.20, s32[16,256]{1,0:T(8,128)} %node_hbm.1, bf16[16,256]{1,0:T(8,128)(2,1)} %emis_hbm.1, f32[64,128]{1,0:T(8,128)} %bitcast.16, s32[1,96]{1,0:T(1,128)} %bitcast.24, s32[1,96]{1,0:T(1,128)} %bitcast.25, bf16[16,4,256]{2,1,0:T(4,128)(2,1)} %frac_hbm.1, ...), custom_call_target="tpu_custom_call" | custom-call | tf_op jit(solution)/shard_map/pallas_call | solution.py:605
  79.0 1.4 %copy.19 = f32[8192]{0:T(1024)} copy(f32[8192]{0:T(1024)} %bitcast.19) | data formatting | bytes 65536
  80.4 1.3 %copy.20 = f32[16,256]{1,0:T(8,128)} copy(f32[16,256]{1,0:T(8,128)} %get-tuple-element.9) | data formatting | bytes 32768

commit v5 on v3

--- a/solution.py
+++ b/solution.py
@@ -24,6 +24,7 @@
 CONDS = 192
 CPAD = 256
 TURNED = 56
+LATE = 72
 MESH = pl.DeviceIdType.MESH
 F32 = jnp.float32
 BF16 = jnp.bfloat16
@@ -441,7 +442,7 @@
 
     column_peers(send_absorb)
     ab_recv[pl.ds(c, 1)] = ab_send[pl.ds(c, 1)]
-    lax.fori_loop(TURNED, VIEWS, turn, 0, unroll=4)
+    lax.fori_loop(TURNED, LATE, turn, 0, unroll=4)
     drain(frac_all.at[:, others, :], setup_recv.at[2])
     drain(frac_all.at[:, others, :], setup_send.at[2])
     rank_row = iota((CAP, VIEW), 0)
@@ -474,7 +475,15 @@
             prod[:, k, :] = mm(ecol[:, k, :].astype(BF16), vb[k])
             return carry
 
-        lax.fori_loop(0, VIEWS, view, 0, unroll=32)
+        def view_unturned(k, carry):
+            prod[:, k, :] = mm_nt(ecol[:, k, :].astype(BF16), vb[k])
+            return carry
+
+        if it == 0:
+            lax.fori_loop(0, LATE, view, 0, unroll=36)
+            lax.fori_loop(LATE, VIEWS, view_unturned, 0, unroll=24)
+        else:
+            lax.fori_loop(0, VIEWS, view, 0, unroll=32)
         if it == 0:
             drain(ab_recv.at[0 : COLUMNS - 1], setup_recv.at[3])
             drain(ab_recv.at[0 : COLUMNS - 1], setup_send.at[3])
@@ -541,6 +550,7 @@
                     jnp.concatenate(left, axis=1), jnp.concatenate(right, axis=1)
                 )
             esum[...] = weight
+            lax.fori_loop(LATE, VIEWS, turn, 0, unroll=4)
         drain(f_recv.at[it, 0 : PEERS - 1], f_rsem.at[it])
         drain(f_recv.at[it, 0 : PEERS - 1], f_ssem.at[it])
         came = f_recv[it, :, 0, :]

time: 81.4 us -> 81.8 us (level)
  no operation moved by 1% of the time
where the time goes in v5:
time: 81.8 us; the launch traced here: 81.5 us
  Pallas kernels  78.1 us (95%)
  local copies, waits for them, and re-layouts  2.7 us (3%)
    pallas_call x1, Pallas kernels, shards(): pl.pallas_call(kernel, out_shape=(jax.ShapeDtypeStruct((TILES, TILE), F32...  78.1 us
    unnamed x2, local copies, waits for them, and re-layouts  2.7 us

profile of v5, /device:TPU:1, one launch (start us, length us, event | category | flops | bytes accessed | tf_op | source)
XLA Modules:
  0.0 81.5 jit_solution(4384249010380302319)
XLA Ops:
  0.6 78.1 %shard_map.158 = (f32[64,128]{1,0:T(8,128)}, f32[16,256]{1,0:T(8,128)}) custom-call(s32[16,1,256]{2,1,0:T(1,128)} %bitcast.20, s32[16,256]{1,0:T(8,128)} %node_hbm.1, bf16[16,256]{1,0:T(8,128)(2,1)} %emis_hbm.1, f32[64,128]{1,0:T(8,128)} %bitcast.16, s32[1,96]{1,0:T(1,128)} %bitcast.24, s32[1,96]{1,0:T(1,128)} %bitcast.25, bf16[16,4,256]{2,1,0:T(4,128)(2,1)} %frac_hbm.1, ...), custom_call_target="tpu_custom_call" | custom-call | tf_op jit(solution)/shard_map/pallas_call | solution.py:605
  78.8 1.4 %copy.19 = f32[8192]{0:T(1024)} copy(f32[8192]{0:T(1024)} %bitcast.19) | data formatting | bytes 65536
  80.2 1.3 %copy.20 = f32[16,256]{1,0:T(8,128)} copy(f32[16,256]{1,0:T(8,128)} %get-tuple-element.9) | data formatting | bytes 32768
